TPU v7x, 512 devices: a whole 4x8x8 slice. The times are simulated.
512 devices in a mesh: loop: 64 (over z, y_hi, core), rep: 8 (over y_lo, x).
Axes of the slice: x: 4, y: 8 (y_hi: 4, y_lo: 2; y = y_hi * 2 + y_lo), z: 8, core: 2. Of those that a mesh axis runs over, the one named last changes fastest.
Arguments:
- node_feats: bfloat16 [32768, 256], P(('loop', 'rep')), may hold values from -6 to 6
- weight_matrix: bfloat16 [256, 256], replicated, may hold values from -0.375 to 0.375
- tile_values: bfloat16 [32768, 128, 128], P(('loop', 'rep')), may hold values from -0.25 to 0.25
- tile_rows: int32 [32768], P(('loop', 'rep')), may hold values from 0 to 3, as said below
- tile_cols: int32 [32768], P(('loop', 'rep')), may hold values from 0 to 31
- tile_count: int32 [512], P(('loop', 'rep')), may hold values from 1 to 64, as said below
- labelled: int32 [64, 32], P('loop'), may hold values from 0 to 511
- upstream: bfloat16 [32768, 256], P('loop'), may hold values from -6 to 6
Outputs:
- layer_out: bfloat16 [32768, 256], P(('loop', 'rep'))
- grad_feats: bfloat16 [32768, 256], P(('loop', 'rep'))
- grad_weight: float32 [256, 256], replicated
Inputs may be any that keep to these rules, and one draw needn't show every extreme that they name: On each device the first tile_count slots name distinct (tile_rows, tile_cols) positions; later slots are unused. `tile_count`: some device has all 64 slots live.
All inputs are finite; a program needn't handle non-finite values.
Results may differ from a plain program's by a relative error of at most 0.0061.
Values may be sent and summed in bfloat16 or wider, within the bound.
A program may use at most 64 MiB of HBM per device.

v0:
```python
import math

import jax
import jax.numpy as jnp
from jax import lax
from jax.sharding import PartitionSpec as P


def silu_pair(pre_act):
    gate_value = jax.nn.sigmoid(pre_act)
    return (pre_act * gate_value, gate_value * (1.0 + pre_act * (1.0 - gate_value)))


def per_device(
    node_feats, weight_matrix, tile_values, tile_rows, tile_cols, tile_count, labelled, upstream
):
    tiles_here = tile_values.shape[0]
    tile_size = tile_values.shape[1]
    own_rows = node_feats.shape[0]
    width = node_feats.shape[1]
    block_rows = upstream.shape[0]
    row_tiles = block_rows // tile_size
    group = lax.all_gather(node_feats, "loop", axis=0, tiled=True)
    col_tiles = group.shape[0] // tile_size
    group_tiles = group.reshape(col_tiles, tile_size, width)
    step_size = math.gcd(tiles_here, 16)
    live_count = tile_count[0]
    block_count = (live_count + step_size - 1) // step_size

    def slot_block(block_index):
        begin = block_index * step_size
        values = lax.dynamic_slice_in_dim(tile_values, begin, step_size, 0)
        row_ids = lax.dynamic_slice_in_dim(tile_rows, begin, step_size, 0)
        col_ids = lax.dynamic_slice_in_dim(tile_cols, begin, step_size, 0)
        alive = begin + jnp.arange(step_size, dtype=jnp.int32) < live_count
        values = jnp.where(alive[:, None, None], values, jnp.zeros_like(values))
        return (values, row_ids, col_ids)

    def forward_step(block_index, total):
        values, row_ids, col_ids = slot_block(block_index)
        product = jnp.einsum(
            "kij,kjf->kif", values, group_tiles[col_ids], preferred_element_type=jnp.float32
        )
        return total.at[row_ids].add(product)

    partial_sum = lax.fori_loop(
        0, block_count, forward_step, jnp.zeros((row_tiles, tile_size, width), jnp.float32)
    )
    aggregate = lax.psum(partial_sum, "rep").reshape(block_rows, width)
    aggregate_low = aggregate.astype(jnp.bfloat16)
    pre_act = jnp.dot(aggregate_low, weight_matrix, preferred_element_type=jnp.float32)
    activated, slope = silu_pair(pre_act)
    own_start = lax.axis_index("rep") * own_rows
    layer_out = lax.dynamic_slice_in_dim(activated, own_start, own_rows, 0).astype(jnp.bfloat16)
    label_rows = jnp.any(
        labelled[0][:, None] == jnp.arange(block_rows, dtype=jnp.int32)[None, :], axis=0
    )
    grad_pre = (
        upstream.astype(jnp.float32) * slope * label_rows[:, None].astype(jnp.float32)
    ).astype(jnp.bfloat16)
    contract_rows = (((0,), (0,)), ((), ()))
    own_agg = lax.dynamic_slice_in_dim(aggregate_low, own_start, own_rows, 0)
    own_grad = lax.dynamic_slice_in_dim(grad_pre, own_start, own_rows, 0)
    own_term = lax.dot_general(own_agg, own_grad, contract_rows, preferred_element_type=jnp.float32)
    grad_weight = lax.psum(own_term, ("loop", "rep"))
    grad_agg = lax.dot_general(
        grad_pre, weight_matrix, (((1,), (1,)), ((), ())), preferred_element_type=jnp.float32
    )
    grad_agg = grad_agg.astype(jnp.bfloat16).reshape(row_tiles, tile_size, width)

    def backward_step(block_index, total):
        values, row_ids, col_ids = slot_block(block_index)
        product = jnp.einsum(
            "kij,kif->kjf", values, grad_agg[row_ids], preferred_element_type=jnp.float32
        )
        return total.at[col_ids].add(product)

    column_term = lax.fori_loop(
        0, block_count, backward_step, jnp.zeros((col_tiles, tile_size, width), jnp.float32)
    )
    loop_size = lax.axis_size("loop")
    grad_feats = lax.psum_scatter(
        column_term.reshape(loop_size * own_rows, width), "loop", scatter_dimension=0, tiled=True
    )
    return (layer_out, grad_feats.astype(jnp.bfloat16), grad_weight)


def solution(mesh):
    placed = (
        P(("loop", "rep"), None),
        P(),
        P(("loop", "rep"), None, None),
        P(("loop", "rep")),
        P(("loop", "rep")),
        P(("loop", "rep")),
        P("loop", None),
        P("loop", None),
    )
    return jax.shard_map(
        per_device,
        mesh=mesh,
        in_specs=placed,
        out_specs=(P(("loop", "rep"), None), P(("loop", "rep"), None), P()),
        check_vma=False,
    )
```

profile of v0, /device:TPU:1, one launch (start us, length us, event | category | flops | bytes accessed | tf_op | source)
XLA Modules:
  0.0 643.7 jit_solution(12218236439803762235)
XLA Ops:
  9.4 92.1 %all-gather.2.cloned.1.call-done = bf16[4096,256]{1,0:T(8,128)(2,1)} async-done(((bf16[64,256]{1,0:T(8,128)(2,1)}), bf16[4096,256]{1,0:T(8,128)(2,1)}) %all-gather.2.cloned.1.call-update) | async-done | bytes 2097168 | tf_op jit(solution)/shard_map/all_gather | solution.py:23
  101.5 26.2 %while.20 = (s32[]{:T(128)}, f32[4,128,256]{2,1,0:T(8,128)S(1)}, s32[]{:T(128)}, s32[64]{0:T(128)}, s32[]{:T(128)}, /*index=5*/bf16[64,128,128]{2,1,0:T(8,128)(2...) while((s32[]{:T(128)}, f32[4,128,256]{2,1,0:T(8,128)S(1)}, ...), condition=%wide.region_2.3_spmd, body=%wide.region_0.2_spmd.sunk | while | flops 135005312 | bytes 12063379 | solution.py:46
  103.0 3.2 gather_fusion
  106.2 1.9 fusion.32
  108.1 2.2 scatter_fusion
  111.7 3.2 gather_fusion
  114.9 1.9 fusion.32
  116.8 2.2 scatter_fusion
  120.4 3.2 gather_fusion
  123.6 1.9 fusion.32
  125.5 2.2 scatter_fusion
  127.7 30.6 %all-reduce.4 = bf16[4,128,256]{2,1,0:T(8,128)(2,1)S(1)} all-reduce(f32[4,128,256]{2,1,0:T(8,128)S(1)} %get-tuple-element.89), channel_id=1, replica_groups=mesh['loop'=64,'rep'=8] {'rep'}, use_global_device_ids=true, to_apply=%region_3.4 | all-reduce | flops 131072 | bytes 786432 | tf_op jit(solution)/shard_map/psum | solution.py:49
  158.3 1.2 multiply_convert_fusion
  159.8 2.4 broadcast_in_dim.36
  162.3 28.7 %while.21 = (s32[]{:T(128)}, f32[32,128,256]{2,1,0:T(8,128)}, s32[]{:T(128)}, s32[64]{0:T(128)S(1)}, s32[]{:T(128)}, /*index=5*/bf16[64,128,128]{2,1,0:T(8,128)(...) while((s32[]{:T(128)}, f32[32,128,256]{2,1,0:T(8,128)}, ...), condition=%wide.region_7.8_spmd, body=%wide.region_5.7_spmd.sunk | while | flops 135005312 | bytes 14160531 | solution.py:78
  163.1 1.1 constant_dynamic-slice_fusion.2
  165.8 1.5 fusion.35
  167.3 4.5 scatter_fusion.1
  172.6 1.1 constant_dynamic-slice_fusion.2
  173.7 1.0 copy.15
  175.4 1.5 fusion.35
  176.9 4.5 scatter_fusion.1
  182.1 1.1 constant_dynamic-slice_fusion.2
  183.2 1.0 copy.15
  184.9 1.5 fusion.35
  186.4 4.6 scatter_fusion.1
  191.0 1.7 fusion.14
  192.8 1.5 fusion.12
  194.3 167.2 %reduce-scatter.2.cloned.1.call-done = f32[64,256]{1,0:T(8,128)} async-done(((f32[4096,256]{1,0:T(8,128)}), f32[64,256]{1,0:T(8,128)}) %reduce-scatter.2.cloned.1.call-update) | async-done | bytes 65552 | tf_op jit(solution)/shard_map/reduce_scatter | solution.py:82
  361.4 1.5 convert_element_type.36
  362.9 272.6 %all-reduce.3.cloned.1.call-done = f32[256,256]{1,0:T(8,128)} async-done(((f32[256,256]{1,0:T(8,128)}), f32[256,256]{1,0:T(8,128)}) %all-reduce.3.cloned.1.call-update) | async-done | bytes 262160 | tf_op jit(solution)/shard_map/psum | solution.py:65
  635.5 1.7 copy.34
  (44 shorter events, 11.3 us)
Async XLA Ops:
  7.2 151.1 %copy-start = (bf16[256,256]{1,0:T(8,128)(2,1)S(1)}, bf16[256,256]{1,0:T(8,128)(2,1)}, u32[]{:S(2)}) copy-start(bf16[256,256]{1,0:T(8,128)(2,1)} %param.13) | copy-start | bytes 393220
  7.2 94.3 %all-gather.2.cloned.1.call-start = ((), (), s32[]{:S(2)}) async-start(), calls=%async_computation.1 | async-start | bytes 2129920 | tf_op jit(solution)/shard_map/all_gather | solution.py:23
  7.9 353.5 %reduce-scatter.2.cloned.1.call-start = ((), (), s32[]{:S(2)}) async-start(), calls=%async_computation.2 | async-start | bytes 4259840 | tf_op jit(solution)/shard_map/reduce_scatter | solution.py:82
  101.5 56.8 %copy-start.5 = (bf16[512,256]{1,0:T(8,128)(2,1)S(1)}, bf16[512,256]{1,0:T(8,128)(2,1)}, u32[]{:S(2)}) copy-start(bf16[512,256]{1,0:T(8,128)(2,1)} %param.19) | copy-start | bytes 786436
  158.3 4.0 copy-start.1
  159.6 2.7 copy-start.2
  159.8 2.5 copy-start.3
  159.8 2.4 copy-start.4
  191.0 444.5 %all-reduce.3.cloned.1.call-start = ((), (), s32[]{:S(2)}) async-start(), calls=%async_computation.3 | async-start | bytes 524288 | tf_op jit(solution)/shard_map/psum | solution.py:65
Sparse Core Ops, SparseCore 0:
  11.4 90.0 all-gather.1
  191.1 170.2 reduce-scatter.1
  367.2 268.2 all-reduce.2
where the time goes:
time: 645 us; the launch traced here: 644 us
  waiting for transfers between devices  533 us (83%)
  blocking collectives  30.6 us (5%)
  other arithmetic  30.3 us (5%)
  local copies, waits for them, and re-layouts  22 us (3%)
  between operations  14.5 us (2%)
  matrix products  13.4 us (2%)
    psum x1, waiting for transfers between devices, per_device(): grad_weight = lax.psum(own_term, ('loop', 'rep'))  273 us
    reduce_scatter x1, waiting for transfers between devices, per_device(): lax.psum_scatter(column_term.reshape(loop_size * own_rows, width), 'loop'...  167 us
    all_gather x1, waiting for transfers between devices, per_device(): group = lax.all_gather(node_feats, 'loop', axis=0, tiled=True)  92.1 us
    psum x1, blocking collectives, per_device(): aggregate = lax.psum(partial_sum, 'rep').reshape(block_rows, width)  30.6 us
    scatter-add x3, other arithmetic, backward_step(): return total.at[col_ids].add(product)  13.6 us
  transfers between devices with their start and end apart: 3, of which 3 were waited for; matrix products, arithmetic and copies ran while one was open for 1% of the time, Pallas kernels for 0%

commit v1 on v0

v1 whole, which is shorter than its diff:
```python
import jax
import jax.numpy as jnp
from jax import lax
from jax.experimental import pallas as pl
from jax.experimental.pallas import tpu as pltpu
from jax.sharding import PartitionSpec as P

MESH = pl.DeviceIdType.MESH
NZ, NY, NC, NR = 8, 4, 2, 8
ROWS, FEAT, TILE, SLOTS = 64, 256, 128, 64
TEAM, LAB, RT = 512, 32, 4
COLS = NZ * NY
F32, BF16, I32 = jnp.float32, jnp.bfloat16, jnp.int32
CONTRACT_ROWS = (((0,), (0,)), ((), ()))
CONTRACT_LANES = (((1,), (1,)), ((), ()))


def iota(shape, dim):
    return lax.broadcasted_iota(I32, shape, dim)


def to_column(row):
    n = row.shape[1]
    square = jnp.broadcast_to(row, (n, n))
    return jnp.sum(jnp.where(iota((n, n), 0) == iota((n, n), 1), square, 0), axis=1, keepdims=True)


def kernel(
    feats, weight, values, trows, tcols, tcount, lab, upstream,
    layer_out, grad_feats, grad_weight,
    x3, tiles, dense, wv, upv, table_v, table_s, acc, asub, a4, at4, at8,
    stage, rep_in, msg, wpart, cstage, cin, gwbuf,
    local_sem, y_s, y_r, z_s, z_r, c_s, c_r, a_s, a_r, t_s, t_r,
    rep_s, rep_r, m_s, m_r, w_s, w_r, b_s, b_r, v_s, v_r,
):
    loop, rep = lax.axis_index("loop"), lax.axis_index("rep")
    z, yh, c = loop // 8, (loop // 2) % 4, loop % 2

    def at(dz=0, dy=0, dc=0, dr=0):
        nz, ny = lax.rem(z + dz + NZ, NZ), lax.rem(yh + dy + NY, NY)
        nc, nr = lax.rem(c + dc, NC), lax.rem(rep + dr, NR)
        return (nz * 8 + ny * 2 + nc, nr)

    sends = []

    def push(src, dst, ss, rs, to):
        copy = pltpu.make_async_remote_copy(
            src_ref=src, dst_ref=dst, send_sem=ss, recv_sem=rs, device_id=to, device_id_type=MESH
        )
        copy.start()
        sends.append(copy)
        return copy

    loads = [
        pltpu.make_async_copy(values, tiles.at[pl.ds(0, SLOTS)], local_sem.at[0]),
        pltpu.make_async_copy(feats, x3.at[z * NY + yh, pl.ds(c * ROWS, ROWS)], local_sem.at[1]),
        pltpu.make_async_copy(weight, wv, local_sem.at[2]),
        pltpu.make_async_copy(upstream, upv, local_sem.at[3]),
    ]
    for load in loads:
        load.start()

    peers = [at(dz=i) for i in range(1, NZ)]
    peers += [at(dy=i, dc=k) for k in range(2) for i in range(NY) if i + k]
    peers += [at(dr=i) for i in range(1, NR)]
    barrier = pltpu.get_barrier_semaphore()
    for peer in peers:
        pl.semaphore_signal(barrier, inc=1, device_id=peer, device_id_type=MESH)

    pos = to_column(trows[...] * COLS + tcols[...])
    live = iota((SLOTS, 1), 0) < tcount[0, 0]
    hit = (pos == iota((SLOTS, TILE), 1)) & live
    table_v[...] = SLOTS + jnp.sum(jnp.where(hit, iota((SLOTS, TILE), 0) - SLOTS, 0), axis=0, keepdims=True)
    table_copy = pltpu.make_async_copy(table_v, table_s, local_sem.at[4])
    table_copy.start()

    pl.semaphore_wait(barrier, len(peers))

    def shard(dz, dy):
        nz, ny = lax.rem(z + dz + NZ, NZ), lax.rem(yh + dy + NY, NY)
        return x3.at[nz * NY + ny, pl.ds(c * ROWS, ROWS)]

    own = shard(0, 0)
    y_in, up_in, down_in, sib_in = {}, {}, {}, {}
    for jj in (2, 1, 3):
        y_in[jj] = push(feats, own, y_s.at[jj], y_r.at[jj], at(dy=jj))

    def forward(src, block, s, jj):
        pass

    def send_up(src, s, jj):
        up_in[s, jj] = push(src, shard(1 - s, -jj), z_s.at[0, s, jj], z_r.at[0, s, jj], at(dz=1))

    def send_down(src, s, jj):
        down_in[s, jj] = push(src, shard(s - 1, -jj), z_s.at[1, s, jj], z_r.at[1, s, jj], at(dz=-1))

    def send_sib(src, dz, jj):
        i = (dz % NZ) * NY + jj
        sib_in[dz, jj] = push(src, shard(dz, -jj), c_s.at[i], c_r.at[i], at(dc=1))

    send_up(feats, 1, 0)
    send_down(feats, 1, 0)
    send_sib(feats, 0, 0)

    lab_row = lab[...]
    lab_col = to_column(lab_row)
    twice = (lab_col == lab_row) & (iota((LAB, LAB), 1) < iota((LAB, LAB), 0))
    first = jnp.sum(jnp.where(twice, 1, 0), axis=1, keepdims=True) == 0
    pick = jnp.where((lab_col == iota((LAB, TEAM), 1)) & first, 1.0, 0.0).astype(BF16)

    tiles[SLOTS] = jnp.zeros((TILE, TILE), BF16)
    table_copy.wait()
    loads[0].wait()

    def densify(nz, carry):
        for j in range(NY):
            for rt in range(RT):
                slot = table_s[0, rt * COLS + nz * NY + j]
                dense[nz, rt * TILE:(rt + 1) * TILE, j * TILE:(j + 1) * TILE] = tiles[slot]
        rows = jnp.dot(pick, dense[nz], preferred_element_type=F32).astype(BF16)
        for j in range(NY):
            asub[j, nz] = rows[:, j * TILE:(j + 1) * TILE]
        return carry

    lax.fori_loop(0, NZ, densify, 0)
    a_in = {}
    for jj in (2, 1, 3):
        a_in[jj] = push(asub.at[lax.rem(yh + jj, NY)], a4.at[yh], a_s.at[jj], a_r.at[jj], at(dy=jj))
    a4[yh] = asub[yh]

    for jj in (1, 3, 2):
        y_in[jj].wait_recv()
        src = shard(0, -jj)
        send_up(src, 1, jj)
        send_down(src, 1, jj)
        send_sib(src, 0, jj)
    loads[1].wait()

    order = (0, 1, 3, 2)

    def add_block(dz, fresh=False):
        for jj in range(NY):
            sib_in[dz, jj].wait_recv()
        nz = lax.rem(z + dz + NZ, NZ)
        block = x3[pl.ds(nz * NY, NY)].reshape(NY * TILE, FEAT)
        term = jnp.dot(dense[nz], block, preferred_element_type=F32)
        if fresh:
            acc[...] = term
        else:
            acc[...] += term

    for s in range(1, 4):
        for jj in order:
            up_in[s, jj].wait_recv()
            src = shard(-s, -jj)
            if s < 3 or jj in (0, 1):
                send_up(src, s + 1, jj)
            send_sib(src, -s, jj)
            down_in[s, jj].wait_recv()
            src = shard(s, -jj)
            if s < 3 or jj in (2, 3):
                send_down(src, s + 1, jj)
            send_sib(src, s, jj)
        if s == 1:
            add_block(0, fresh=True)
            for jj in range(1, NY):
                a_in[jj].wait_recv()
            for i in range(NZ):
                block = jnp.concatenate([a4[j, i] for j in range(NY)], axis=0)
                at4[i] = block.astype(F32).T.astype(BF16)
            t_in = push(
                at4.at[:, pl.ds((1 - c) * ROWS, ROWS)], at8.at[:, :, pl.ds(c * TILE, TILE)],
                t_s.at[0], t_r.at[0], at(dc=1),
            )
            at8[:, :, pl.ds(pl.multiple_of(c * TILE, TILE), TILE)] = at4[:, pl.ds(pl.multiple_of(c * ROWS, ROWS), ROWS)]
        else:
            add_block(1 - s)
            add_block(s - 1)
    for jj in order:
        (up_in if jj in (0, 1) else down_in)[4, jj].wait_recv()
        send_sib(shard(-4, -jj), -4, jj)
    add_block(-3)
    add_block(3)
    add_block(-4)

    low = acc[...].astype(BF16)
    picked = jnp.dot(pick, low, preferred_element_type=F32).astype(BF16)
    for i in range(NR):
        stage[i, 0:ROWS] = low[i * ROWS:(i + 1) * ROWS]
        stage[i, ROWS:ROWS + LAB] = picked
    rep_in_c = {}
    for d in (6, 2, 5, 7, 3, 1, 4):
        rep_in_c[d] = push(stage.at[lax.rem(rep + d, NR)], rep_in.at[d], rep_s.at[d], rep_r.at[d], at(dr=d))
    loads[2].wait()
    loads[3].wait()
    w = wv[...]
    up_lab = jnp.dot(pick, upv[...], preferred_element_type=F32)
    total = stage[rep].astype(F32)
    for d in (4, 1, 3, 7, 5, 2, 6):
        rep_in_c[d].wait_recv()
        total += rep_in[d].astype(F32)
    agg = total.astype(BF16)
    pre = jnp.dot(agg, w, preferred_element_type=F32)
    gate = jax.nn.sigmoid(pre)
    layer_out[...] = (pre * gate)[0:ROWS].astype(BF16)
    pre_l, gate_l = pre[ROWS:], gate[ROWS:]
    slope = gate_l * (1.0 + pre_l * (1.0 - gate_l))
    mine = c * NY + yh
    msg[mine, :, 0:FEAT] = (up_lab * slope).astype(BF16)
    chunk = (iota((FEAT, TILE), 0) == rep * LAB + iota((FEAT, TILE), 1)) & (iota((FEAT, TILE), 1) < LAB)
    msg[mine, :, FEAT:] = jnp.dot(
        agg[ROWS:], jnp.where(chunk, 1.0, 0.0).astype(BF16), preferred_element_type=F32
    ).astype(BF16)
    m_in = []
    for dy, dc in ((2, 1), (2, 0), (1, 1), (3, 1), (1, 0), (3, 0), (0, 1)):
        i = dc * NY + dy
        m_in.append(push(msg.at[mine], msg.at[mine], m_s.at[i], m_r.at[i], at(dy=dy, dc=dc)))
    t_in.wait_recv()
    for copy in reversed(m_in):
        copy.wait_recv()

    grad_pre = msg[:, :, 0:FEAT].reshape(NC * NY * LAB, FEAT)
    agg_chunk = msg[:, :, FEAT:].reshape(NC * NY * LAB, TILE)
    part = lax.dot_general(agg_chunk, grad_pre, CONTRACT_ROWS, preferred_element_type=F32)
    wpart[z] = part[0:LAB].astype(BF16)
    w_in, b_in = [], []
    for d in (4, 3, 5, 2, 6, 1, 7):
        w_in.append(push(wpart.at[z], wpart.at[z], w_s.at[d], w_r.at[d], at(dz=d)))
    grad_agg = lax.dot_general(grad_pre, w, CONTRACT_LANES, preferred_element_type=F32).astype(BF16)
    term = jnp.dot(at8[...].reshape(NZ * ROWS, NC * NY * LAB), grad_agg, preferred_element_type=F32)
    cstage[...] = term.astype(BF16).reshape(NZ, ROWS, FEAT)
    for d in (4, 3, 5, 2, 6, 1, 7):
        b_in.append(push(cstage.at[lax.rem(z + d, NZ)], cin.at[d], b_s.at[d], b_r.at[d], at(dz=d)))
    for copy in reversed(w_in):
        copy.wait_recv()
    chunk_sum = wpart[0].astype(F32)
    for i in range(1, NZ):
        chunk_sum += wpart[i].astype(F32)
    gwbuf[rep] = chunk_sum
    v_in = []
    for d in (6, 2, 5, 7, 3, 1, 4):
        v_in.append(push(gwbuf.at[rep], gwbuf.at[rep], v_s.at[d], v_r.at[d], at(dr=d)))
    total = cstage[z].astype(F32)
    for d, copy in zip((7, 1, 6, 2, 5, 3, 4), reversed(b_in)):
        copy.wait_recv()
        total += cin[d].astype(F32)
    grad_feats[...] = total.astype(BF16)
    for copy in reversed(v_in):
        copy.wait_recv()
    grad_weight[...] = gwbuf[...].reshape(FEAT, FEAT)
    for copy in sends:
        copy.wait_send()


def per_device(
    node_feats, weight_matrix, tile_values, tile_rows, tile_cols, tile_count, labelled, upstream
):
    any_space = pl.BlockSpec(memory_space=pl.ANY)
    vmem = pl.BlockSpec(memory_space=pltpu.VMEM)
    smem = pl.BlockSpec(memory_space=pltpu.SMEM)
    dma = pltpu.SemaphoreType.DMA
    return pl.pallas_call(
        kernel,
        name="graph_layer",
        out_shape=(
            jax.ShapeDtypeStruct((ROWS, FEAT), BF16),
            jax.ShapeDtypeStruct((ROWS, FEAT), BF16),
            jax.ShapeDtypeStruct((FEAT, FEAT), F32),
        ),
        in_specs=[any_space, any_space, any_space, vmem, vmem, smem, vmem, any_space],
        out_specs=(vmem, vmem, vmem),
        scratch_shapes=[
            pltpu.VMEM((COLS, TILE, FEAT), BF16),
            pltpu.VMEM((SLOTS + 1, TILE, TILE), BF16),
            pltpu.VMEM((NZ, TEAM, NY * TILE), BF16),
            pltpu.VMEM((FEAT, FEAT), BF16),
            pltpu.VMEM((TEAM, FEAT), BF16),
            pltpu.VMEM((1, TILE), I32),
            pltpu.SMEM((1, TILE), I32),
            pltpu.VMEM((TEAM, FEAT), F32),
            pltpu.VMEM((NY, NZ, LAB, TILE), BF16),
            pltpu.VMEM((NY, NZ, LAB, TILE), BF16),
            pltpu.VMEM((NZ, TILE, TILE), BF16),
            pltpu.VMEM((NZ, ROWS, NC * TILE), BF16),
            pltpu.VMEM((NR, ROWS + LAB, FEAT), BF16),
            pltpu.VMEM((NR, ROWS + LAB, FEAT), BF16),
            pltpu.VMEM((NC * NY, LAB, FEAT + TILE), BF16),
            pltpu.VMEM((NZ, LAB, FEAT), BF16),
            pltpu.VMEM((NZ, ROWS, FEAT), BF16),
            pltpu.VMEM((NZ, ROWS, FEAT), BF16),
            pltpu.VMEM((NR, LAB, FEAT), F32),
            dma((5,)),
            dma((4,)), dma((4,)), dma((2, 5, 4)), dma((2, 5, 4)), dma((32,)), dma((32,)),
            dma((4,)), dma((4,)), dma((1,)), dma((1,)),
            dma((8,)), dma((8,)), dma((8,)), dma((8,)), dma((8,)), dma((8,)),
            dma((8,)), dma((8,)), dma((8,)), dma((8,)),
        ],
        compiler_params=pltpu.CompilerParams(
            collective_id=0, has_side_effects=True, vmem_limit_bytes=40 * 2**20
        ),
    )(
        node_feats, weight_matrix, tile_values, tile_rows.reshape(1, SLOTS), tile_cols.reshape(1, SLOTS),
        tile_count.reshape(1, 1), labelled, upstream,
    )


def solution(mesh):
    placed = (
        P(("loop", "rep"), None),
        P(),
        P(("loop", "rep"), None, None),
        P(("loop", "rep")),
        P(("loop", "rep")),
        P(("loop", "rep")),
        P("loop", None),
        P("loop", None),
    )
    return jax.shard_map(
        per_device,
        mesh=mesh,
        in_specs=placed,
        out_specs=(P(("loop", "rep"), None), P(("loop", "rep"), None), P()),
        check_vma=False,
    )
```

time: 645 us -> 75 us (0.12)
  waiting for transfers between devices: 533 us -> 0 us
  Pallas kernels: 0 us -> 65.3 us
  blocking collectives: 30.6 us -> 0 us
  other arithmetic: 30.3 us -> 0 us
  local copies, waits for them, and re-layouts: 22 us -> 8.09 us
  matrix products: 13.4 us -> 0 us
  between operations: 14.5 us -> 1.3 us
    psum x1 -> x0, waiting for transfers between devices: 273 us -> none  [per_device(): grad_weight = lax.psum(own_term, ('loop', 'rep'))]
    reduce_scatter x1 -> x0, waiting for transfers between devices: 167 us -> none  [per_device(): lax.psum_scatter(column_term.reshape(loop_size * own_rows, width), 'loop'...]
    all_gather x1 -> x0, waiting for transfers between devices: 92.1 us -> none  [per_device(): group = lax.all_gather(node_feats, 'loop', axis=0, tiled=True)]
    pallas_call x0 -> x1, Pallas kernels: none -> 65.3 us  [per_device(): pl.pallas_call(kernel, name='graph_layer', out_shape=(jax.ShapeDtypeStruc...]
    psum x1 -> x0, blocking collectives: 30.6 us -> none  [per_device(): aggregate = lax.psum(partial_sum, 'rep').reshape(block_rows, width)]
    scatter-add x6 -> x0, other arithmetic: 20.1 us -> none  [the longest x3 13.6 us: backward_step(): return total.at[col_ids].add(product)]
    dot_general x9 -> x0, matrix products: 13.4 us -> none  [the longest x3 5.6 us: forward_step(): jnp.einsum('kij,kjf->kif', values, group_tiles[col_ids], preferred_elemen...]
    gather x6 -> x0, local copies, waits for them, and re-layouts: 11.5 us -> none  [the longest x3 9.62 us: forward_step(): group_tiles[col_ids]]
  transfers between devices with their start and end apart: 3 -> 0, of which waited for: 3 -> 0; matrix products, arithmetic and copies ran while one was open for 1% -> 0% of each run, Pallas kernels for 0% -> 0%
where the time goes in v1:
time: 75 us; the launch traced here: 74.7 us
  Pallas kernels  65.3 us (87%)
  local copies, waits for them, and re-layouts  8.09 us (11%)
  between operations  1.3 us (2%)
    pallas_call x1, Pallas kernels, per_device(): pl.pallas_call(kernel, name='graph_layer', out_shape=(jax.ShapeDtypeStruc...  65.3 us
    unnamed x17, local copies, waits for them, and re-layouts  8.09 us

profile of v1, /device:TPU:1, one launch (start us, length us, event | category | flops | bytes accessed | tf_op | source)
XLA Modules:
  0.0 74.7 jit_solution(1047902411384187439)
XLA Ops:
  1.3 0.0 copy-start
  1.3 1.6 %copy-done = bf16[64,128,128]{2,1,0:T(8,128)(2,1)S(1)} copy-done((bf16[64,128,128]{2,1,0:T(8,128)(2,1)S(1)}, bf16[64,128,128]{2,1,0:T(8,128)(2,1)}, u32[]{:S(2)}) %copy-start) | copy-done | bytes 2097176
  2.9 0.0 copy-start.1
  2.9 0.9 %copy-done.1 = bf16[512,256]{1,0:T(8,128)(2,1)S(1)} copy-done((bf16[512,256]{1,0:T(8,128)(2,1)S(1)}, bf16[512,256]{1,0:T(8,128)(2,1)}, u32[]{:S(2)}) %copy-start.1) | copy-done | bytes 262168
  3.8 0.0 copy-start.2
  3.8 0.9 %copy-done.2 = bf16[256,256]{1,0:T(8,128)(2,1)S(1)} copy-done((bf16[256,256]{1,0:T(8,128)(2,1)S(1)}, bf16[256,256]{1,0:T(8,128)(2,1)}, u32[]{:S(2)}) %copy-start.2) | copy-done | bytes 131096
  4.7 0.0 copy-start.3
  4.7 0.8 %copy-done.3 = bf16[64,256]{1,0:T(8,128)(2,1)S(1)} copy-done((bf16[64,256]{1,0:T(8,128)(2,1)S(1)}, bf16[64,256]{1,0:T(8,128)(2,1)}, u32[]{:S(2)}) %copy-start.3) | copy-done | bytes 32792
  5.5 0.0 copy-start.4
  5.5 0.7 copy-done.4
  6.1 0.0 copy-start.5
  6.1 0.7 copy-done.5
  6.8 0.0 copy-start.6
  6.8 0.7 copy-done.6
  7.5 65.3 %graph_layer.1 = (bf16[64,256]{1,0:T(8,128)(2,1)S(1)}, bf16[64,256]{1,0:T(8,128)(2,1)S(1)}, f32[256,256]{1,0:T(8,128)S(1)}) custom-call(bf16[64,256]{1,0:T(8,128)(2,1)S(1)} %copy-done.3, bf16[256,256]{1,0:T(8,128)(2,1)S(1)} %copy-done.2, bf16[64,128,128]{2,1,0:T(8,128)(2,1)S(1)} %copy-done, s32[1,64]{1,0:T(1,128)S(1)} %bitcast.4, s32[1,64]{1,0:T(1,128)S(1)} %bitcast.5, ...), custom_call_target="tpu_custom_call" | custom-call | tf_op jit(solution)/shard_map/graph_layer/pallas_call | solution.py:262
  72.7 0.6 copy.15
  73.3 0.6 copy.16
  74.0 0.7 copy.17
Async XLA Ops:
  1.3 1.6 %copy-start = (bf16[64,128,128]{2,1,0:T(8,128)(2,1)S(1)}, bf16[64,128,128]{2,1,0:T(8,128)(2,1)}, u32[]{:S(2)}) copy-start(bf16[64,128,128]{2,1,0:T(8,128)(2,1)} %values.1) | copy-start | bytes 6291460
  2.9 0.9 %copy-start.1 = (bf16[512,256]{1,0:T(8,128)(2,1)S(1)}, bf16[512,256]{1,0:T(8,128)(2,1)}, u32[]{:S(2)}) copy-start(bf16[512,256]{1,0:T(8,128)(2,1)} %upstream.1) | copy-start | bytes 786436
  3.8 0.9 %copy-start.2 = (bf16[256,256]{1,0:T(8,128)(2,1)S(1)}, bf16[256,256]{1,0:T(8,128)(2,1)}, u32[]{:S(2)}) copy-start(bf16[256,256]{1,0:T(8,128)(2,1)} %weight.1) | copy-start | bytes 393220
  4.7 0.8 %copy-start.3 = (bf16[64,256]{1,0:T(8,128)(2,1)S(1)}, bf16[64,256]{1,0:T(8,128)(2,1)}, u32[]{:S(2)}) copy-start(bf16[64,256]{1,0:T(8,128)(2,1)} %feats.1) | copy-start | bytes 98308
  5.5 0.7 copy-start.4
  6.1 0.7 copy-start.5
  6.8 0.7 copy-start.6

commit v2 on v1

v2 whole, which is shorter than its diff:
```python
import jax
import jax.numpy as jnp
from jax import lax
from jax.experimental import pallas as pl
from jax.experimental.pallas import tpu as pltpu
from jax.sharding import PartitionSpec as P

MESH = pl.DeviceIdType.MESH
NZ, NY, NC, NR = 8, 4, 2, 8
ROWS, FEAT, TILE, SLOTS = 64, 256, 128, 64
TEAM, LAB, RT = 512, 32, 4
REP_HALF = (ROWS + LAB) // 2
HALF = LAB // NC
COLS = NZ * NY
F32, BF16, I32 = jnp.float32, jnp.bfloat16, jnp.int32
CONTRACT_ROWS = (((0,), (0,)), ((), ()))
CONTRACT_LANES = (((1,), (1,)), ((), ()))


def iota(shape, dim):
    return lax.broadcasted_iota(I32, shape, dim)


def to_column(row):
    n = row.shape[1]
    square = jnp.broadcast_to(row, (n, n))
    return jnp.sum(jnp.where(iota((n, n), 0) == iota((n, n), 1), square, 0), axis=1, keepdims=True)


def kernel(
    feats, weight, values, trows_h, tcols_h, tcount_h, lab_h, upstream,
    layer_out, grad_feats, grad_weight,
    x3, tiles, dense, wv, upv, trows, tcols, lab, tcount, table_v, table_s, acc, asub, a4, at4, at8,
    stage, rep_in, relay_in, msg, wpart, part_v, cstage, cin, gwbuf, z_relay,
    local_sem, y_s, y_r, h_s, h_r, z_s, z_r, c_s, c_r, l_s, l_r, a_s, a_r, t_s, t_r,
    q_s, q_r, rep_s, rep_r, m_s, m_r, w_s, w_r, b_s, b_r, f_s, f_r, v_s, v_r,
):
    loop, rep = lax.axis_index("loop"), lax.axis_index("rep")
    z, yh, c = loop // 8, (loop // 2) % 4, loop % 2

    def at(dz=0, dy=0, dc=0, dr=0):
        nz, ny = lax.rem(z + dz + NZ, NZ), lax.rem(yh + dy + NY, NY)
        nc, nr = lax.rem(c + dc, NC), lax.rem(rep + dr, NR)
        return (nz * 8 + ny * 2 + nc, nr)

    sends = []

    def push(src, dst, ss, rs, to):
        copy = pltpu.make_async_remote_copy(
            src_ref=src, dst_ref=dst, send_sem=ss, recv_sem=rs, device_id=to, device_id_type=MESH
        )
        copy.start()
        sends.append(copy)
        return copy

    small = [
        pltpu.make_async_copy(trows_h, trows, local_sem.at[5]),
        pltpu.make_async_copy(tcols_h, tcols, local_sem.at[6]),
        pltpu.make_async_copy(tcount_h, tcount, local_sem.at[7]),
        pltpu.make_async_copy(lab_h, lab, local_sem.at[8]),
    ]
    for load in small:
        load.start()
    loads = [
        pltpu.make_async_copy(values, tiles.at[pl.ds(0, SLOTS)], local_sem.at[0]),
        pltpu.make_async_copy(feats, x3.at[z * NY + yh, pl.ds(c * ROWS, ROWS)], local_sem.at[1]),
        pltpu.make_async_copy(weight, wv, local_sem.at[2]),
        pltpu.make_async_copy(upstream, upv, local_sem.at[3]),
    ]

    peers = [at(dz=i) for i in (4, 3, 5, 2, 6, 1, 7)]
    peers += [at(dy=i) for i in (2, 1, 3)] + [at(dc=1)]
    peers += [at(dr=i) for i in (6, 2, 5, 7, 3, 1, 4)]
    barrier = pltpu.get_barrier_semaphore()
    for peer in peers:
        pl.semaphore_signal(barrier, inc=1, device_id=peer, device_id_type=MESH)
    for load in loads:
        load.start()
    pl.semaphore_wait(barrier, len(peers))

    step = 1 - 2 * c

    def z_at(k):
        return lax.rem(z + k + NZ, NZ)

    def chip_block(k, jj):
        return x3.at[z_at(k) * NY + lax.rem(yh - jj + NY, NY)]

    def half_block(jj):
        return chip_block(0, jj).at[pl.ds(c * ROWS, ROWS)]

    y_in, half_in, z_in, sib_in, last_in = {}, {}, {}, {}, []

    def send_ring(s, jj):
        block = chip_block(-step * (s - 1), jj)
        if s == 4:
            block = block.at[pl.ds(c * ROWS, ROWS)]
        z_in[s, jj] = push(block, block, z_s.at[s, jj], z_r.at[s, jj], at(dz=step))

    def ring(s, jj):
        z_in[s, jj].wait_recv()
        if s < 4:
            send_ring(s + 1, jj)

    def send_sib(s):
        block = x3.at[pl.ds(z_at(-step * s) * NY, NY)]
        sib_in[s] = push(block, block, c_s.at[s], c_r.at[s], at(dc=1))

    def from_y(jj):
        y_in[jj].wait_recv()
        half_in[jj] = push(half_block(jj), half_block(jj), h_s.at[jj], h_r.at[jj], at(dc=1))

    def from_sib(jj):
        half_in[jj].wait_recv()
        send_ring(1, jj)

    half_in[0] = push(feats, half_block(0), h_s.at[0], h_r.at[0], at(dc=1))
    for jj in (2, 1, 3):
        y_in[jj] = push(feats, half_block(0), y_s.at[jj], y_r.at[jj], at(dy=jj))

    loads[1].wait()
    from_sib(0)

    for load in small:
        load.wait()
    pos = to_column(trows[...] * COLS + tcols[...])
    live = iota((SLOTS, 1), 0) < tcount[0]
    hit = (pos == iota((SLOTS, TILE), 1)) & live
    table_v[...] = SLOTS + jnp.sum(jnp.where(hit, iota((SLOTS, TILE), 0) - SLOTS, 0), axis=0, keepdims=True)
    table_copy = pltpu.make_async_copy(table_v, table_s, local_sem.at[4])
    table_copy.start()

    lab_row = lab[...]
    lab_col = to_column(lab_row)
    twice = (lab_col == lab_row) & (iota((LAB, LAB), 1) < iota((LAB, LAB), 0))
    first = jnp.sum(jnp.where(twice, 1, 0), axis=1, keepdims=True) == 0
    pick = jnp.where((lab_col == iota((LAB, TEAM), 1)) & first, 1.0, 0.0).astype(BF16)

    tiles[SLOTS] = jnp.zeros((TILE, TILE), BF16)

    def densify(nz, carry):
        for j in range(NY):
            for rt in range(RT):
                slot = table_s[0, rt * COLS + nz * NY + j]
                dense[nz, rt * TILE:(rt + 1) * TILE, j * TILE:(j + 1) * TILE] = tiles[slot]
        rows = jnp.dot(pick, dense[nz], preferred_element_type=F32).astype(BF16)
        for j in range(NY):
            asub[j, nz] = rows[:, j * TILE:(j + 1) * TILE]
        return carry

    def add_block(k, fresh=False):
        nz = z_at(k)
        block = x3[pl.ds(nz * NY, NY)].reshape(NY * TILE, FEAT)
        term = jnp.dot(dense[nz], block, preferred_element_type=F32)
        if fresh:
            acc[...] = term
        else:
            acc[...] += term

    loads[0].wait()
    table_copy.wait()
    lax.fori_loop(0, 3, densify, 0)
    from_y(1)
    from_y(3)
    ring(1, 0)
    from_sib(1)
    from_sib(3)
    from_y(2)
    lax.fori_loop(3, 5, densify, 0)
    from_sib(2)
    ring(2, 0)
    lax.fori_loop(5, NZ, densify, 0)
    a_in = {}
    for jj in (2, 1, 3):
        a_in[jj] = push(asub.at[lax.rem(yh + jj, NY)], a4.at[yh], a_s.at[jj], a_r.at[jj], at(dy=jj))
    a4[yh] = asub[yh]
    ring(1, 1)
    ring(1, 3)
    ring(3, 0)
    ring(1, 2)
    send_sib(1)
    add_block(0, fresh=True)
    for jj in (1, 3, 2):
        ring(2, jj)
    send_sib(2)
    add_block(-step)
    sib_in[1].wait_recv()
    add_block(step)
    for jj in (1, 3, 2):
        ring(3, jj)
    send_sib(3)
    add_block(-2 * step)
    sib_in[2].wait_recv()
    add_block(2 * step)
    for jj in (0, 1, 3, 2):
        ring(4, jj)
        block = chip_block(4, jj).at[pl.ds(c * ROWS, ROWS)]
        last_in.append(push(block, block, l_s.at[jj], l_r.at[jj], at(dc=1)))
    add_block(-3 * step)
    sib_in[3].wait_recv()
    add_block(3 * step)
    for copy in last_in:
        copy.wait_recv()
    add_block(4)

    low = acc[...].astype(BF16)
    picked = jnp.dot(pick, low, preferred_element_type=F32).astype(BF16)
    for i in range(NR):
        stage[i, 0:ROWS] = low[i * ROWS:(i + 1) * ROWS]
        stage[i, ROWS:ROWS + LAB] = picked
    x, yl = rep % 4, rep // 4

    def target(dx, dyl):
        return lax.rem(yl + dyl, 2) * 4 + lax.rem(x + dx + 4, 4)

    halves = (pl.ds(0, REP_HALF), pl.ds(REP_HALF, REP_HALF))
    relay, rep_arrivals = {}, []
    for dyl in (1, 0):
        for side, dx in enumerate((1, -1)):
            relay[side, dyl] = push(
                stage.at[target(2, dyl), halves[side]], relay_in.at[side, dyl],
                q_s.at[side, dyl], q_r.at[side, dyl], (loop, target(dx, 0)),
            )

    def send_rep(dx, dyl, part, i):
        to = target(dx, dyl)
        rep_arrivals.append(push(
            stage.at[to, part], rep_in.at[dyl * 3 + dx + 1, part], rep_s.at[i], rep_r.at[i], (loop, to)
        ))

    send_rep(0, 1, pl.ds(0, ROWS + LAB), 0)
    for dyl in (1, 0):
        for side, dx in enumerate((1, -1)):
            send_rep(dx, dyl, halves[1 - side], 1 + dyl * 2 + side)
    for dyl in (1, 0):
        for side, dx in enumerate((1, -1)):
            relay[side, dyl].wait_recv()
            to, part = target(dx, dyl), halves[side]
            merged = stage[to, part].astype(F32) + relay_in[side, dyl].astype(F32)
            stage[to, part] = merged.astype(BF16)
            send_rep(dx, dyl, part, 5 + dyl * 2 + side)
    gather_sends = list(sends)
    for jj in range(1, NY):
        a_in[jj].wait_recv()
    for i in range(NZ):
        block = jnp.concatenate([a4[j, i] for j in range(NY)], axis=0)
        at4[i] = block.astype(F32).T.astype(BF16)
    t_in = push(
        at4.at[:, pl.ds((1 - c) * ROWS, ROWS)], at8.at[:, :, pl.ds(c * TILE, TILE)],
        t_s.at[0], t_r.at[0], at(dc=1),
    )
    at8[:, :, pl.ds(pl.multiple_of(c * TILE, TILE), TILE)] = at4[:, pl.ds(pl.multiple_of(c * ROWS, ROWS), ROWS)]
    for copy in gather_sends:
        copy.wait_send()
    loads[2].wait()
    loads[3].wait()
    w = wv[...]
    up_lab = jnp.dot(pick, upv[...], preferred_element_type=F32)
    total = stage[rep].astype(F32)
    for copy in rep_arrivals:
        copy.wait_recv()
    for i in (0, 2, 3, 4, 5):
        total += rep_in[i].astype(F32)
    agg = total.astype(BF16)
    pre = jnp.dot(agg, w, preferred_element_type=F32)
    gate = jax.nn.sigmoid(pre)
    layer_out[...] = (pre * gate)[0:ROWS].astype(BF16)
    pre_l, gate_l = pre[ROWS:], gate[ROWS:]
    slope = gate_l * (1.0 + pre_l * (1.0 - gate_l))
    mine = c * NY + yh
    msg[mine, :, 0:FEAT] = (up_lab * slope).astype(BF16)
    chunk = (iota((FEAT, TILE), 0) == rep * LAB + iota((FEAT, TILE), 1)) & (iota((FEAT, TILE), 1) < LAB)
    msg[mine, :, FEAT:] = jnp.dot(
        agg[ROWS:], jnp.where(chunk, 1.0, 0.0).astype(BF16), preferred_element_type=F32
    ).astype(BF16)
    m_in, m_sib = {}, []
    for dy in (2, 1, 3):
        m_in[dy] = push(msg.at[mine], msg.at[mine], m_s.at[dy], m_r.at[dy], at(dy=dy))

    def pass_msg(dy):
        slot = msg.at[c * NY + lax.rem(yh - dy + NY, NY)]
        m_sib.append(push(slot, slot, m_s.at[4 + dy], m_r.at[4 + dy], at(dc=1)))

    pass_msg(0)
    t_in.wait_recv()
    for dy in (1, 3, 2):
        m_in[dy].wait_recv()
        pass_msg(dy)
    for copy in m_sib:
        copy.wait_recv()

    grad_pre = msg[:, :, 0:FEAT].reshape(NC * NY * LAB, FEAT)
    agg_chunk = msg[:, :, FEAT:].reshape(NC * NY * LAB, TILE)
    part = lax.dot_general(agg_chunk, grad_pre, CONTRACT_ROWS, preferred_element_type=F32)
    part_v[...] = part[0:LAB]
    wpart[z] = part_v[pl.ds(pl.multiple_of(c * HALF, HALF), HALF)].astype(BF16)
    w_in, b_in = [], []
    for d in (4, 3, 5, 2, 6, 1, 7):
        w_in.append(push(wpart.at[z], wpart.at[z], w_s.at[d], w_r.at[d], at(dz=d)))
    grad_agg = lax.dot_general(grad_pre, w, CONTRACT_LANES, preferred_element_type=F32).astype(BF16)
    term = jnp.dot(at8[...].reshape(NZ * ROWS, NC * NY * LAB), grad_agg, preferred_element_type=F32)
    cstage[...] = term.astype(BF16).reshape(NZ, ROWS, FEAT)
    top, bottom = pl.ds(0, ROWS // 2), pl.ds(ROWS // 2, ROWS // 2)
    far = [
        push(cstage.at[z_at(4), top], z_relay.at[0], f_s.at[0], f_r.at[0], at(dz=3)),
        push(cstage.at[z_at(4), bottom], z_relay.at[1], f_s.at[1], f_r.at[1], at(dz=-3)),
    ]
    for d in (3, -3, 2, -2):
        b_in.append(push(cstage.at[z_at(d)], cin.at[d % NZ], b_s.at[d % NZ], b_r.at[d % NZ], at(dz=d)))
    b_in.append(push(cstage.at[z_at(1), bottom], cin.at[1, bottom], b_s.at[1], b_r.at[1], at(dz=1)))
    b_in.append(push(cstage.at[z_at(-1), top], cin.at[7, top], b_s.at[7], b_r.at[7], at(dz=-1)))
    for copy in reversed(w_in):
        copy.wait_recv()
    chunk_sum = wpart[0].astype(F32)
    for i in range(1, NZ):
        chunk_sum += wpart[i].astype(F32)
    gwbuf[rep, c] = chunk_sum.astype(BF16)
    v_in = []
    for d in (6, 2, 5, 7, 3, 1, 4):
        v_in.append(push(gwbuf.at[rep, c], gwbuf.at[rep, c], v_s.at[d], v_r.at[d], at(dr=d)))
    for i, (d, part) in enumerate(((1, top), (-1, bottom))):
        far[i].wait_recv()
        merged = cstage[z_at(d), part].astype(F32) + z_relay[i].astype(F32)
        cstage[z_at(d), part] = merged.astype(BF16)
        b_in.append(push(cstage.at[z_at(d), part], cin.at[d % NZ, part], f_s.at[2 + i], f_r.at[2 + i], at(dz=d)))
    for copy in reversed(v_in):
        copy.wait_recv()
    v_sib = push(gwbuf.at[:, c], gwbuf.at[:, c], v_s.at[0], v_r.at[0], at(dc=1))
    total = cstage[z].astype(F32)
    for copy in b_in:
        copy.wait_recv()
    for d in (1, 2, 3, 5, 6, 7):
        total += cin[d].astype(F32)
    grad_feats[...] = total.astype(BF16)
    for copy in sends[len(gather_sends):]:
        copy.wait_send()
    v_sib.wait_recv()
    grad_weight[...] = gwbuf[...].astype(F32).reshape(FEAT, FEAT)


def write_out(layer_in, feats_in, weight_in, layer_out, grad_feats, grad_weight):
    layer_out[...] = layer_in[...]
    grad_feats[...] = feats_in[...]
    grad_weight[...] = weight_in[...]


def per_device(
    node_feats, weight_matrix, tile_values, tile_rows, tile_cols, tile_count, labelled, upstream
):
    hbm = pl.BlockSpec(memory_space=pl.ANY)
    vmem = pl.BlockSpec(memory_space=pltpu.VMEM)
    dma = pltpu.SemaphoreType.DMA
    shapes = (
        jax.ShapeDtypeStruct((ROWS, FEAT), BF16),
        jax.ShapeDtypeStruct((ROWS, FEAT), BF16),
        jax.ShapeDtypeStruct((FEAT, FEAT), F32),
    )
    results = pl.pallas_call(
        kernel,
        name="graph_layer",
        out_shape=shapes,
        in_specs=[hbm] * 8,
        out_specs=(vmem, vmem, vmem),
        scratch_shapes=[
            pltpu.VMEM((COLS, TILE, FEAT), BF16),
            pltpu.VMEM((SLOTS + 1, TILE, TILE), BF16),
            pltpu.VMEM((NZ, TEAM, NY * TILE), BF16),
            pltpu.VMEM((FEAT, FEAT), BF16),
            pltpu.VMEM((TEAM, FEAT), BF16),
            pltpu.VMEM((1, SLOTS), I32),
            pltpu.VMEM((1, SLOTS), I32),
            pltpu.VMEM((1, LAB), I32),
            pltpu.SMEM((1,), I32),
            pltpu.VMEM((1, TILE), I32),
            pltpu.SMEM((1, TILE), I32),
            pltpu.VMEM((TEAM, FEAT), F32),
            pltpu.VMEM((NY, NZ, LAB, TILE), BF16),
            pltpu.VMEM((NY, NZ, LAB, TILE), BF16),
            pltpu.VMEM((NZ, TILE, TILE), BF16),
            pltpu.VMEM((NZ, ROWS, NC * TILE), BF16),
            pltpu.VMEM((NR, ROWS + LAB, FEAT), BF16),
            pltpu.VMEM((6, ROWS + LAB, FEAT), BF16),
            pltpu.VMEM((2, 2, REP_HALF, FEAT), BF16),
            pltpu.VMEM((NC * NY, LAB, FEAT + TILE), BF16),
            pltpu.VMEM((NZ, HALF, FEAT), BF16),
            pltpu.VMEM((LAB, FEAT), F32),
            pltpu.VMEM((NZ, ROWS, FEAT), BF16),
            pltpu.VMEM((NZ, ROWS, FEAT), BF16),
            pltpu.VMEM((NR, NC, HALF, FEAT), BF16),
            pltpu.VMEM((2, ROWS // 2, FEAT), BF16),
            dma((9,)),
            dma((4,)), dma((4,)), dma((4,)), dma((4,)), dma((5, 4)), dma((5, 4)), dma((4,)), dma((4,)), dma((4,)), dma((4,)),
            dma((4,)), dma((4,)), dma((1,)), dma((1,)),
            dma((2, 2)), dma((2, 2)), dma((9,)), dma((9,)), dma((8,)), dma((8,)), dma((8,)), dma((8,)),
            dma((8,)), dma((8,)), dma((4,)), dma((4,)), dma((8,)), dma((8,)),
        ],
        compiler_params=pltpu.CompilerParams(
            collective_id=0, has_side_effects=True, vmem_limit_bytes=60 * 2**20
        ),
    )(
        node_feats, weight_matrix, tile_values, tile_rows.reshape(1, SLOTS), tile_cols.reshape(1, SLOTS),
        tile_count, labelled, upstream,
    )
    return pl.pallas_call(
        write_out,
        name="write_out",
        out_shape=shapes,
        in_specs=[vmem] * 3,
        out_specs=(vmem,) * 3,
        compiler_params=pltpu.CompilerParams(vmem_limit_bytes=60 * 2**20),
    )(*results)


def solution(mesh):
    placed = (
        P(("loop", "rep"), None),
        P(),
        P(("loop", "rep"), None, None),
        P(("loop", "rep")),
        P(("loop", "rep")),
        P(("loop", "rep")),
        P("loop", None),
        P("loop", None),
    )
    return jax.shard_map(
        per_device,
        mesh=mesh,
        in_specs=placed,
        out_specs=(P(("loop", "rep"), None), P(("loop", "rep"), None), P()),
        check_vma=False,
    )
```

time: 75 us -> 67.9 us (0.905)
  local copies, waits for them, and re-layouts: 8.09 us -> 0 us
  Pallas kernels: 65.3 us -> 66.5 us
    unnamed x17 -> x0, local copies, waits for them, and re-layouts: 8.09 us -> none
    pallas_call x1 -> x2, Pallas kernels: 65.3 us -> 66.5 us  [the longest x1 64.7 us: per_device(): pl.pallas_call(kernel, name='graph_layer', out_shape=shapes, in_specs=[hb...]
where the time goes in v2:
time: 67.9 us; the launch traced here: 67.7 us
  Pallas kernels  66.5 us (98%)
  between operations  1.29 us (2%)
    pallas_call x1, Pallas kernels, per_device(): pl.pallas_call(kernel, name='graph_layer', out_shape=shapes, in_specs=[hb...  64.7 us
    pallas_call x1, Pallas kernels, per_device(): pl.pallas_call(write_out, name='write_out', out_shape=shapes, in_specs=[v...  1.72 us

profile of v2, /device:TPU:1, one launch (start us, length us, event | category | flops | bytes accessed | tf_op | source)
XLA Modules:
  0.0 67.7 jit_solution(14361222788042232060)
XLA Ops:
  1.3 64.7 %graph_layer.1 = (bf16[64,256]{1,0:T(8,128)(2,1)}, bf16[64,256]{1,0:T(8,128)(2,1)}, f32[256,256]{1,0:T(8,128)}) custom-call(bf16[64,256]{1,0:T(8,128)(2,1)} %feats.1, bf16[256,256]{1,0:T(8,128)(2,1)} %weight.1, bf16[64,128,128]{2,1,0:T(8,128)(2,1)} %values.1, s32[1,64]{1,0:T(1,128)} %bitcast.2, s32[1,64]{1,0:T(1,128)} %bitcast.3, s32[1]{0:T(128)S(6)} %copy.11.tcount_h, ...), custom_call_target="tpu_custom_call" | custom-call | tf_op jit(solution)/shard_map/graph_layer/pallas_call | solution.py:358
  66.0 1.7 %write_out.1 = (bf16[64,256]{1,0:T(8,128)(2,1)}, bf16[64,256]{1,0:T(8,128)(2,1)}, f32[256,256]{1,0:T(8,128)}) custom-call(bf16[64,256]{1,0:T(8,128)(2,1)} %get-tuple-element.6.layer_in, bf16[64,256]{1,0:T(8,128)(2,1)} %get-tuple-element.7.feats_in, f32[256,256]{1,0:T(8,128)} %get-tuple-element.8.weight_in), custom_call_target="tpu_custom_call" | custom-call | tf_op jit(solution)/shard_map/write_out/pallas_call | solution.py:404

commit v3 on v2

v3 whole, which is shorter than its diff:
```python
import jax
import jax.numpy as jnp
from jax import lax
from jax.experimental import pallas as pl
from jax.experimental.pallas import tpu as pltpu
from jax.sharding import PartitionSpec as P

MESH = pl.DeviceIdType.MESH
NZ, NY, NC, NR = 8, 4, 2, 8
ROWS, FEAT, TILE, SLOTS = 64, 256, 128, 64
TEAM, LAB, RT = 512, 32, 4
REP_HALF = ROWS + LAB
HALF = LAB // NC
COLS = NZ * NY
F32, BF16, I32 = jnp.float32, jnp.bfloat16, jnp.int32
CONTRACT_ROWS = (((0,), (0,)), ((), ()))
CONTRACT_LANES = (((1,), (1,)), ((), ()))


def iota(shape, dim):
    return lax.broadcasted_iota(I32, shape, dim)


def to_column(row):
    n = row.shape[1]
    square = jnp.broadcast_to(row, (n, n))
    return jnp.sum(jnp.where(iota((n, n), 0) == iota((n, n), 1), square, 0), axis=1, keepdims=True)


def kernel(
    feats, weight, values, trows_h, tcols_h, tcount_h, lab_h, upstream,
    layer_out, grad_feats, grad_weight,
    x3, tiles, tiles_sib, dense, wv, upv, trows, tcols, lab, tcount, info, info_sib, table_s, acc, asub, a4, at4, at8,
    stage, rep_in, relay_in, msg, chunk, wpart, ypart, part_v, cstage, cin, gwbuf, z_relay,
    local_sem, y_s, y_r, h_s, h_r, z_s, z_r, a_s, a_r, t_s, t_r,
    q_s, q_r, rep_s, rep_r, m_s, m_r, w_s, w_r, u_s, u_r, b_s, b_r, f_s, f_r, v_s, v_r,
):
    loop, rep = lax.axis_index("loop"), lax.axis_index("rep")
    z, yh, c = loop // 8, (loop // 2) % 4, loop % 2

    def at(dz=0, dy=0, dc=0, dr=0):
        nz, ny = lax.rem(z + dz + NZ, NZ), lax.rem(yh + dy + NY, NY)
        nc, nr = lax.rem(c + dc, NC), lax.rem(rep + dr, NR)
        return (nz * 8 + ny * 2 + nc, nr)

    sends = []

    def push(src, dst, ss, rs, to):
        copy = pltpu.make_async_remote_copy(
            src_ref=src, dst_ref=dst, send_sem=ss, recv_sem=rs, device_id=to, device_id_type=MESH
        )
        copy.start()
        sends.append(copy)
        return copy

    small = [
        pltpu.make_async_copy(trows_h, trows, local_sem.at[5]),
        pltpu.make_async_copy(tcols_h, tcols, local_sem.at[6]),
        pltpu.make_async_copy(tcount_h, tcount, local_sem.at[7]),
        pltpu.make_async_copy(lab_h, lab, local_sem.at[8]),
    ]
    for load in small:
        load.start()
    lanes = pl.ds(pl.multiple_of(c * TILE, TILE), TILE)
    other_lanes = pl.ds(pl.multiple_of((1 - c) * TILE, TILE), TILE)
    own_rows = pl.ds(pl.multiple_of(c * ROWS, ROWS), ROWS)
    own_half = x3.at[z * NY + yh, own_rows]
    loads = [
        pltpu.make_async_copy(values, tiles.at[pl.ds(0, SLOTS)], local_sem.at[0]),
        pltpu.make_async_copy(feats.at[:, lanes], own_half, local_sem.at[1]),
        pltpu.make_async_copy(weight, wv, local_sem.at[2]),
        pltpu.make_async_copy(upstream, upv, local_sem.at[3]),
    ]

    peers = [at(dz=i) for i in (4, 3, 5, 2, 6, 1, 7)]
    peers += [at(dy=i, dc=k) for i in (2, 1, 3) for k in range(NC)] + [at(dc=1)]
    peers += [at(dr=i) for i in (6, 2, 5, 7, 3, 1, 4)]
    x, yl = rep % 4, rep // 4

    def target(dx, dyl):
        return lax.rem(yl + dyl, 2) * 4 + lax.rem(x + dx + 4, 4)

    near = ((1, 1), (-1, 1), (0, 1), (1, 0), (-1, 0))
    peers += [(at(dc=1)[0], target(dx, dyl)) for dx, dyl in near]
    barrier = pltpu.get_barrier_semaphore()
    for peer in peers:
        pl.semaphore_signal(barrier, inc=1, device_id=peer, device_id_type=MESH)
    for load in loads:
        load.start()
    pl.semaphore_wait(barrier, len(peers))

    def z_at(k):
        return lax.rem(z + k + NZ, NZ)

    def chip_block(k, jj):
        return x3.at[z_at(k) * NY + lax.rem(yh - jj + NY, NY)]

    y_in, up_in, down_in = {}, {}, {}

    def send_up(s, jj):
        block = chip_block(1 - s, jj)
        if s == 4:
            block = block.at[pl.ds(0, ROWS)]
        up_in[s, jj] = push(block, block, z_s.at[0, s, jj], z_r.at[0, s, jj], at(dz=1))

    def send_down(s, jj):
        block = chip_block(s - 1, jj)
        if s == 4:
            block = block.at[pl.ds(ROWS, ROWS)]
        down_in[s, jj] = push(block, block, z_s.at[1, s, jj], z_r.at[1, s, jj], at(dz=-1))

    def send_ring(s, jj):
        send_up(s, jj)
        send_down(s, jj)

    def ring(s, jj):
        up_in[s, jj].wait_recv()
        if s < 4:
            send_up(s + 1, jj)
        down_in[s, jj].wait_recv()
        if s < 4:
            send_down(s + 1, jj)

    def from_y(jj):
        y_in[jj, 0].wait_recv()
        y_in[jj, 1].wait_recv()
        send_ring(1, jj)

    sib_own = push(feats.at[:, other_lanes], own_half, h_s.at[0], h_r.at[0], at(dc=1))
    for jj in (2, 1, 3):
        y_in[jj, 0] = push(feats.at[:, lanes], own_half, y_s.at[jj, 0], y_r.at[jj, 0], at(dy=jj))
        y_in[jj, 1] = push(feats.at[:, other_lanes], own_half, y_s.at[jj, 1], y_r.at[jj, 1], at(dy=jj, dc=1))
    tiles_in = push(values, tiles_sib.at[pl.ds(0, SLOTS)], h_s.at[1], h_r.at[1], at(dc=1))

    for load in small:
        load.wait()
    pos = to_column(trows[...] * COLS + tcols[...])
    live = iota((SLOTS, 1), 0) < tcount[0]
    hit = (pos == iota((SLOTS, TILE), 1)) & live
    info[...] = jnp.zeros_like(info)
    info[0:1] = SLOTS + jnp.sum(jnp.where(hit, iota((SLOTS, TILE), 0) - SLOTS, 0), axis=0, keepdims=True)
    info[1:2, 0:LAB] = lab[...]
    info_in = push(info, info_sib, h_s.at[2], h_r.at[2], at(dc=1))
    table_copy = pltpu.make_async_copy(info, table_s.at[0], local_sem.at[4])
    table_copy.start()

    loads[1].wait()
    sib_own.wait_recv()
    send_ring(1, 0)

    def picker(lab_row):
        lab_col = to_column(lab_row)
        twice = (lab_col == lab_row) & (iota((LAB, LAB), 1) < iota((LAB, LAB), 0))
        first = jnp.sum(jnp.where(twice, 1, 0), axis=1, keepdims=True) == 0
        return jnp.where((lab_col == iota((LAB, TEAM), 1)) & first, 1.0, 0.0).astype(BF16)

    pick = picker(lab[...])
    tiles[SLOTS] = jnp.zeros((TILE, TILE), BF16)
    tiles_sib[SLOTS] = jnp.zeros((TILE, TILE), BF16)

    def densify(team, held, nz):
        for j in range(NY):
            for rt in range(RT):
                slot = table_s[team, 0, rt * COLS + nz * NY + j]
                dense[team, nz, rt * TILE:(rt + 1) * TILE, j * TILE:(j + 1) * TILE] = held[slot]

    def densify_own(nz, carry):
        densify(0, tiles, nz)
        rows = jnp.dot(pick, dense[0, nz], preferred_element_type=F32).astype(BF16)
        for j in range(NY):
            asub[j, nz] = rows[:, j * TILE:(j + 1) * TILE]
        return carry

    def densify_sib(nz, carry):
        densify(1, tiles_sib, nz)
        return carry

    def add_block(k, fresh=False):
        nz = z_at(k)
        block = x3[pl.ds(nz * NY, NY)].reshape(NY * TILE, TILE)
        for team in range(NC):
            term = jnp.dot(dense[team, nz], block, preferred_element_type=F32)
            if fresh:
                acc[team] = term
            else:
                acc[team] += term

    loads[0].wait()
    table_copy.wait()
    lax.fori_loop(0, 4, densify_own, 0)
    from_y(1)
    from_y(3)
    ring(1, 0)
    from_y(2)
    lax.fori_loop(4, NZ, densify_own, 0)
    a_in = {}
    for jj in (2, 1, 3):
        a_in[jj] = push(asub.at[lax.rem(yh + jj, NY)], a4.at[yh], a_s.at[jj], a_r.at[jj], at(dy=jj))
    ring(1, 1)
    ring(1, 3)
    ring(2, 0)
    ring(1, 2)
    a4[yh] = asub[yh]
    info_in.wait_recv()
    sib_table = pltpu.make_async_copy(info_sib, table_s.at[1], local_sem.at[9])
    sib_table.start()
    pick_sib = picker(info_sib[1:2, 0:LAB])
    ring(2, 1)
    ring(2, 3)
    ring(3, 0)
    ring(2, 2)
    sib_table.wait()
    tiles_in.wait_recv()
    lax.fori_loop(0, NZ, densify_sib, 0)
    ring(3, 1)
    ring(3, 3)
    ring(3, 2)
    add_block(0, fresh=True)
    add_block(1)
    add_block(-1)
    add_block(2)
    add_block(-2)
    add_block(3)
    add_block(-3)
    for jj in (0, 1, 3, 2):
        ring(4, jj)
    add_block(4)

    for team, rows in enumerate((pick, pick_sib)):
        low = acc[team].astype(BF16)
        picked = jnp.dot(rows, low, preferred_element_type=F32).astype(BF16)
        base = team * REP_HALF
        for i in range(NR):
            stage[i, base:base + ROWS] = low[i * ROWS:(i + 1) * ROWS]
            stage[i, base + ROWS:base + REP_HALF] = picked
    halves = (pl.ds(0, REP_HALF), pl.ds(REP_HALF, REP_HALF))
    relay, rep_arrivals = {}, []
    for dyl in (1, 0):
        for side, dx in enumerate((1, -1)):
            relay[side, dyl] = push(
                stage.at[target(2, dyl), halves[side]], relay_in.at[side, dyl],
                q_s.at[side, dyl], q_r.at[side, dyl], (loop, target(dx, 0)),
            )

    def send_rep(dx, dyl, side):
        to, slot = target(dx, dyl), dyl * 3 + dx + 1
        rep_arrivals.append(push(
            stage.at[to, halves[side]], rep_in.at[slot, :, lanes],
            rep_s.at[slot, side], rep_r.at[slot, side], (at(dc=side)[0], to),
        ))

    send_rep(0, 1, 0)
    send_rep(0, 1, 1)
    for dyl in (1, 0):
        for side, dx in enumerate((1, -1)):
            send_rep(dx, dyl, 1 - side)
    send_rep(0, 0, 1)
    rep_in[1, :, lanes] = stage[rep, 0:REP_HALF]
    for dyl in (1, 0):
        for side, dx in enumerate((1, -1)):
            relay[side, dyl].wait_recv()
            to, part = target(dx, dyl), halves[side]
            merged = stage[to, part].astype(F32) + relay_in[side, dyl].astype(F32)
            stage[to, part] = merged.astype(BF16)
            send_rep(dx, dyl, side)
    gather_sends = list(sends)
    for jj in range(1, NY):
        a_in[jj].wait_recv()
    for i in range(NZ):
        block = jnp.concatenate([a4[j, i] for j in range(NY)], axis=0)
        at4[i] = block.astype(F32).T.astype(BF16)
    t_in = push(
        at4.at[:, pl.ds((1 - c) * ROWS, ROWS)], at8.at[:, :, pl.ds(c * TILE, TILE)],
        t_s.at[0], t_r.at[0], at(dc=1),
    )
    at8[:, :, pl.ds(pl.multiple_of(c * TILE, TILE), TILE)] = at4[:, pl.ds(pl.multiple_of(c * ROWS, ROWS), ROWS)]
    for copy in gather_sends:
        copy.wait_send()
    loads[2].wait()
    loads[3].wait()
    w = wv[...]
    up_lab = jnp.dot(pick, upv[...], preferred_element_type=F32)
    for copy in rep_arrivals:
        copy.wait_recv()
    total = rep_in[0].astype(F32)
    for i in range(1, 6):
        total += rep_in[i].astype(F32)
    agg = total.astype(BF16)
    pre = jnp.dot(agg, w, preferred_element_type=F32)
    gate = jax.nn.sigmoid(pre)
    layer_out[...] = (pre * gate)[0:ROWS].astype(BF16)
    pre_l, gate_l = pre[ROWS:], gate[ROWS:]
    slope = gate_l * (1.0 + pre_l * (1.0 - gate_l))
    mine = c * NY + yh
    msg[mine] = (up_lab * slope).astype(BF16)
    m_in, m_sib = {}, []
    for dy in (2, 1, 3):
        m_in[dy] = push(msg.at[mine], msg.at[mine], m_s.at[dy], m_r.at[dy], at(dy=dy))

    def pass_msg(dy):
        slot = msg.at[c * NY + lax.rem(yh - dy + NY, NY)]
        m_sib.append(push(slot, slot, m_s.at[4 + dy], m_r.at[4 + dy], at(dc=1)))

    pass_msg(0)
    chosen = (iota((FEAT, TILE), 0) == rep * LAB + iota((FEAT, TILE), 1)) & (iota((FEAT, TILE), 1) < LAB)
    chunk[c] = jnp.dot(agg[ROWS:], jnp.where(chosen, 1.0, 0.0).astype(BF16), preferred_element_type=F32).astype(BF16)
    chunk_in = push(chunk.at[c], chunk.at[c], m_s.at[0], m_r.at[0], at(dc=1))
    m_sib[0].wait_recv()
    chunk_in.wait_recv()
    part = lax.dot_general(
        chunk[...].reshape(NC * LAB, TILE), jnp.concatenate([msg[yh], msg[NY + yh]], axis=0),
        CONTRACT_ROWS, preferred_element_type=F32,
    )
    part_v[...] = part[0:LAB]
    wpart[z] = part_v[pl.ds(pl.multiple_of(c * HALF, HALF), HALF)].astype(BF16)
    w_in, b_in = [], []
    for d in (4, 3, 5, 2, 6, 1, 7):
        w_in.append(push(wpart.at[z], wpart.at[z], w_s.at[d], w_r.at[d], at(dz=d)))
    t_in.wait_recv()
    for dy in (1, 3, 2):
        m_in[dy].wait_recv()
        pass_msg(dy)
    for copy in m_sib[1:]:
        copy.wait_recv()

    grad_pre = msg[...].reshape(NC * NY * LAB, FEAT)
    grad_agg = lax.dot_general(grad_pre, w, CONTRACT_LANES, preferred_element_type=F32).astype(BF16)
    term = jnp.dot(at8[...].reshape(NZ * ROWS, NC * NY * LAB), grad_agg, preferred_element_type=F32)
    cstage[...] = term.astype(BF16).reshape(NZ, ROWS, FEAT)
    top, bottom = pl.ds(0, ROWS // 2), pl.ds(ROWS // 2, ROWS // 2)
    far = [
        push(cstage.at[z_at(4), top], z_relay.at[0], f_s.at[0], f_r.at[0], at(dz=3)),
        push(cstage.at[z_at(4), bottom], z_relay.at[1], f_s.at[1], f_r.at[1], at(dz=-3)),
    ]
    for d in (3, -3, 2, -2):
        b_in.append(push(cstage.at[z_at(d)], cin.at[d % NZ], b_s.at[d % NZ], b_r.at[d % NZ], at(dz=d)))
    b_in.append(push(cstage.at[z_at(1), bottom], cin.at[1, bottom], b_s.at[1], b_r.at[1], at(dz=1)))
    b_in.append(push(cstage.at[z_at(-1), top], cin.at[7, top], b_s.at[7], b_r.at[7], at(dz=-1)))
    for copy in reversed(w_in):
        copy.wait_recv()
    chunk_sum = wpart[0].astype(F32)
    for i in range(1, NZ):
        chunk_sum += wpart[i].astype(F32)
    ypart[yh, c] = chunk_sum.astype(BF16)
    u_in = []
    for dy, dc in ((2, 1), (2, 0), (1, 1), (3, 1), (1, 0), (3, 0), (0, 1)):
        u_in.append(push(
            ypart.at[yh, c], ypart.at[yh, c], u_s.at[dc * NY + dy], u_r.at[dc * NY + dy], at(dy=dy, dc=dc)
        ))
    for copy in u_in:
        copy.wait_recv()
    chunk_sum = ypart[0].astype(F32)
    for i in range(1, NY):
        chunk_sum += ypart[i].astype(F32)
    gwbuf[rep] = chunk_sum.astype(BF16)
    v_in = []
    for d in (6, 2, 5, 7, 3, 1, 4):
        v_in.append(push(gwbuf.at[rep], gwbuf.at[rep], v_s.at[d], v_r.at[d], at(dr=d)))
    for i, (d, part) in enumerate(((1, top), (-1, bottom))):
        far[i].wait_recv()
        merged = cstage[z_at(d), part].astype(F32) + z_relay[i].astype(F32)
        cstage[z_at(d), part] = merged.astype(BF16)
        b_in.append(push(cstage.at[z_at(d), part], cin.at[d % NZ, part], f_s.at[2 + i], f_r.at[2 + i], at(dz=d)))
    total = cstage[z].astype(F32)
    for copy in b_in:
        copy.wait_recv()
    for d in (1, 2, 3, 5, 6, 7):
        total += cin[d].astype(F32)
    grad_feats[...] = total.astype(BF16)
    for copy in sends[len(gather_sends):]:
        copy.wait_send()
    for copy in reversed(v_in):
        copy.wait_recv()
    grad_weight[...] = gwbuf[...].astype(F32).reshape(FEAT, FEAT)


def write_out(layer_in, feats_in, weight_in, layer_out, grad_feats, grad_weight):
    layer_out[...] = layer_in[...]
    grad_feats[...] = feats_in[...]
    grad_weight[...] = weight_in[...]


def per_device(
    node_feats, weight_matrix, tile_values, tile_rows, tile_cols, tile_count, labelled, upstream
):
    hbm = pl.BlockSpec(memory_space=pl.ANY)
    vmem = pl.BlockSpec(memory_space=pltpu.VMEM)
    dma = pltpu.SemaphoreType.DMA
    shapes = (
        jax.ShapeDtypeStruct((ROWS, FEAT), BF16),
        jax.ShapeDtypeStruct((ROWS, FEAT), BF16),
        jax.ShapeDtypeStruct((FEAT, FEAT), F32),
    )
    results = pl.pallas_call(
        kernel,
        name="graph_layer",
        out_shape=shapes,
        in_specs=[hbm] * 8,
        out_specs=(vmem, vmem, vmem),
        scratch_shapes=[
            pltpu.VMEM((COLS, TILE, TILE), BF16),
            pltpu.VMEM((SLOTS + 1, TILE, TILE), BF16),
            pltpu.VMEM((SLOTS + 1, TILE, TILE), BF16),
            pltpu.VMEM((NC, NZ, TEAM, NY * TILE), BF16),
            pltpu.VMEM((FEAT, FEAT), BF16),
            pltpu.VMEM((TEAM, FEAT), BF16),
            pltpu.VMEM((1, SLOTS), I32),
            pltpu.VMEM((1, SLOTS), I32),
            pltpu.VMEM((1, LAB), I32),
            pltpu.SMEM((1,), I32),
            pltpu.VMEM((8, TILE), I32),
            pltpu.VMEM((8, TILE), I32),
            pltpu.SMEM((NC, 8, TILE), I32),
            pltpu.VMEM((NC, TEAM, TILE), F32),
            pltpu.VMEM((NY, NZ, LAB, TILE), BF16),
            pltpu.VMEM((NY, NZ, LAB, TILE), BF16),
            pltpu.VMEM((NZ, TILE, TILE), BF16),
            pltpu.VMEM((NZ, ROWS, NC * TILE), BF16),
            pltpu.VMEM((NR, NC * REP_HALF, TILE), BF16),
            pltpu.VMEM((6, REP_HALF, FEAT), BF16),
            pltpu.VMEM((2, 2, REP_HALF, TILE), BF16),
            pltpu.VMEM((NC * NY, LAB, FEAT), BF16),
            pltpu.VMEM((NC, LAB, TILE), BF16),
            pltpu.VMEM((NZ, HALF, FEAT), BF16),
            pltpu.VMEM((NY, NC, HALF, FEAT), BF16),
            pltpu.VMEM((LAB, FEAT), F32),
            pltpu.VMEM((NZ, ROWS, FEAT), BF16),
            pltpu.VMEM((NZ, ROWS, FEAT), BF16),
            pltpu.VMEM((NR, NC, HALF, FEAT), BF16),
            pltpu.VMEM((2, ROWS // 2, FEAT), BF16),
            dma((10,)),
            dma((4, 2)), dma((4, 2)), dma((4,)), dma((4,)), dma((2, 5, 4)), dma((2, 5, 4)),
            dma((4,)), dma((4,)), dma((1,)), dma((1,)),
            dma((2, 2)), dma((2, 2)), dma((6, 2)), dma((6, 2)), dma((8,)), dma((8,)), dma((8,)), dma((8,)), dma((8,)), dma((8,)),
            dma((8,)), dma((8,)), dma((4,)), dma((4,)), dma((8,)), dma((8,)),
        ],
        compiler_params=pltpu.CompilerParams(
            collective_id=0, has_side_effects=True, vmem_limit_bytes=60 * 2**20
        ),
    )(
        node_feats, weight_matrix, tile_values, tile_rows.reshape(1, SLOTS), tile_cols.reshape(1, SLOTS),
        tile_count, labelled, upstream,
    )
    return pl.pallas_call(
        write_out,
        name="write_out",
        out_shape=shapes,
        in_specs=[vmem] * 3,
        out_specs=(vmem,) * 3,
        compiler_params=pltpu.CompilerParams(vmem_limit_bytes=60 * 2**20),
    )(*results)


def solution(mesh):
    placed = (
        P(("loop", "rep"), None),
        P(),
        P(("loop", "rep"), None, None),
        P(("loop", "rep")),
        P(("loop", "rep")),
        P(("loop", "rep")),
        P("loop", None),
        P("loop", None),
    )
    return jax.shard_map(
        per_device,
        mesh=mesh,
        in_specs=placed,
        out_specs=(P(("loop", "rep"), None), P(("loop", "rep"), None), P()),
        check_vma=False,
    )
```

time: 67.9 us -> 63.8 us (0.940)
  Pallas kernels: 66.5 us -> 62.3 us
    pallas_call x1, Pallas kernels: 64.7 us -> 60.6 us  [per_device(): pl.pallas_call(kernel, name='graph_layer', out_shape=shapes, in_specs=[hb...]
where the time goes in v3:
time: 63.8 us; the launch traced here: 63.6 us
  Pallas kernels  62.3 us (98%)
  between operations  1.29 us (2%)
    pallas_call x1, Pallas kernels, per_device(): pl.pallas_call(kernel, name='graph_layer', out_shape=shapes, in_specs=[hb...  60.6 us
    pallas_call x1, Pallas kernels, per_device(): pl.pallas_call(write_out, name='write_out', out_shape=shapes, in_specs=[v...  1.72 us

profile of v3, /device:TPU:1, one launch (start us, length us, event | category | flops | bytes accessed | tf_op | source)
XLA Modules:
  0.0 63.6 jit_solution(15570543175784290081)
XLA Ops:
  1.3 60.6 %graph_layer.1 = (bf16[64,256]{1,0:T(8,128)(2,1)}, bf16[64,256]{1,0:T(8,128)(2,1)}, f32[256,256]{1,0:T(8,128)}) custom-call(bf16[64,256]{1,0:T(8,128)(2,1)} %feats.1, bf16[256,256]{1,0:T(8,128)(2,1)} %weight.1, bf16[64,128,128]{2,1,0:T(8,128)(2,1)} %values.1, s32[1,64]{1,0:T(1,128)} %bitcast.2, s32[1,64]{1,0:T(1,128)} %bitcast.3, s32[1]{0:T(128)S(6)} %copy.11.tcount_h, ...), custom_call_target="tpu_custom_call" | custom-call | tf_op jit(solution)/shard_map/graph_layer/pallas_call | solution.py:394
  61.9 1.7 %write_out.1 = (bf16[64,256]{1,0:T(8,128)(2,1)}, bf16[64,256]{1,0:T(8,128)(2,1)}, f32[256,256]{1,0:T(8,128)}) custom-call(bf16[64,256]{1,0:T(8,128)(2,1)} %get-tuple-element.6.layer_in, bf16[64,256]{1,0:T(8,128)(2,1)} %get-tuple-element.7.feats_in, f32[256,256]{1,0:T(8,128)} %get-tuple-element.8.weight_in), custom_call_target="tpu_custom_call" | custom-call | tf_op jit(solution)/shard_map/write_out/pallas_call | solution.py:444

commit v4 on v3

--- a/solution.py
+++ b/solution.py
@@ -31,7 +31,7 @@
     feats, weight, values, trows_h, tcols_h, tcount_h, lab_h, upstream,
     layer_out, grad_feats, grad_weight,
     x3, tiles, tiles_sib, dense, wv, upv, trows, tcols, lab, tcount, info, info_sib, table_s, acc, asub, a4, at4, at8,
-    stage, rep_in, relay_in, msg, chunk, wpart, ypart, part_v, cstage, cin, gwbuf, z_relay,
+    stage, rep_in, total_v, relay_in, msg, chunk, wpart, ypart, part_v, cstage, cin, gwbuf, z_relay,
     local_sem, y_s, y_r, h_s, h_r, z_s, z_r, a_s, a_r, t_s, t_r,
     q_s, q_r, rep_s, rep_r, m_s, m_r, w_s, w_r, u_s, u_r, b_s, b_r, f_s, f_r, v_s, v_r,
 ):
@@ -97,17 +97,19 @@
 
     y_in, up_in, down_in = {}, {}, {}
 
+    step = 1 - 2 * c
+
     def send_up(s, jj):
-        block = chip_block(1 - s, jj)
+        block = chip_block(step * (1 - s), jj)
         if s == 4:
             block = block.at[pl.ds(0, ROWS)]
-        up_in[s, jj] = push(block, block, z_s.at[0, s, jj], z_r.at[0, s, jj], at(dz=1))
+        up_in[s, jj] = push(block, block, z_s.at[0, s, jj], z_r.at[0, s, jj], at(dz=step))
 
     def send_down(s, jj):
-        block = chip_block(s - 1, jj)
+        block = chip_block(step * (s - 1), jj)
         if s == 4:
             block = block.at[pl.ds(ROWS, ROWS)]
-        down_in[s, jj] = push(block, block, z_s.at[1, s, jj], z_r.at[1, s, jj], at(dz=-1))
+        down_in[s, jj] = push(block, block, z_s.at[1, s, jj], z_r.at[1, s, jj], at(dz=-step))
 
     def send_ring(s, jj):
         send_up(s, jj)
@@ -127,7 +129,7 @@
         send_ring(1, jj)
 
     sib_own = push(feats.at[:, other_lanes], own_half, h_s.at[0], h_r.at[0], at(dc=1))
-    for jj in (2, 1, 3):
+    for jj in (1, 3, 2):
         y_in[jj, 0] = push(feats.at[:, lanes], own_half, y_s.at[jj, 0], y_r.at[jj, 0], at(dy=jj))
         y_in[jj, 1] = push(feats.at[:, other_lanes], own_half, y_s.at[jj, 1], y_r.at[jj, 1], at(dy=jj, dc=1))
     tiles_in = push(values, tiles_sib.at[pl.ds(0, SLOTS)], h_s.at[1], h_r.at[1], at(dc=1))
@@ -207,13 +209,15 @@
     pick_sib = picker(info_sib[1:2, 0:LAB])
     ring(2, 1)
     ring(2, 3)
+    sib_table.wait()
+    tiles_in.wait_recv()
+    lax.fori_loop(0, 2, densify_sib, 0)
     ring(3, 0)
     ring(2, 2)
-    sib_table.wait()
-    tiles_in.wait_recv()
-    lax.fori_loop(0, NZ, densify_sib, 0)
+    lax.fori_loop(2, 5, densify_sib, 0)
     ring(3, 1)
     ring(3, 3)
+    lax.fori_loop(5, NZ, densify_sib, 0)
     ring(3, 2)
     add_block(0, fresh=True)
     add_block(1)
@@ -236,28 +240,31 @@
     halves = (pl.ds(0, REP_HALF), pl.ds(REP_HALF, REP_HALF))
     relay, rep_arrivals = {}, []
     for dyl in (1, 0):
-        for side, dx in enumerate((1, -1)):
+        for side, dx in ((1, -1),):
             relay[side, dyl] = push(
                 stage.at[target(2, dyl), halves[side]], relay_in.at[side, dyl],
                 q_s.at[side, dyl], q_r.at[side, dyl], (loop, target(dx, 0)),
             )
 
     def send_rep(dx, dyl, side):
-        to, slot = target(dx, dyl), dyl * 3 + dx + 1
+        to, slot = target(dx, dyl), dyl * 4 + dx + 1
         rep_arrivals.append(push(
             stage.at[to, halves[side]], rep_in.at[slot, :, lanes],
             rep_s.at[slot, side], rep_r.at[slot, side], (at(dc=side)[0], to),
         ))
 
+    send_rep(2, 1, 0)
+    send_rep(2, 0, 0)
     send_rep(0, 1, 0)
     send_rep(0, 1, 1)
     for dyl in (1, 0):
         for side, dx in enumerate((1, -1)):
             send_rep(dx, dyl, 1 - side)
+        send_rep(1, dyl, 0)
     send_rep(0, 0, 1)
     rep_in[1, :, lanes] = stage[rep, 0:REP_HALF]
     for dyl in (1, 0):
-        for side, dx in enumerate((1, -1)):
+        for side, dx in ((1, -1),):
             relay[side, dyl].wait_recv()
             to, part = target(dx, dyl), halves[side]
             merged = stage[to, part].astype(F32) + relay_in[side, dyl].astype(F32)
@@ -283,8 +290,11 @@
     for copy in rep_arrivals:
         copy.wait_recv()
     total = rep_in[0].astype(F32)
-    for i in range(1, 6):
+    for i in (1, 2, 4, 5, 6):
         total += rep_in[i].astype(F32)
+    total_v[...] = total
+    total_v[:, lanes] += rep_in[3, :, lanes].astype(F32) + rep_in[7, :, lanes].astype(F32)
+    total = total_v[...]
     agg = total.astype(BF16)
     pre = jnp.dot(agg, w, preferred_element_type=F32)
     gate = jax.nn.sigmoid(pre)
@@ -313,7 +323,7 @@
     )
     part_v[...] = part[0:LAB]
     wpart[z] = part_v[pl.ds(pl.multiple_of(c * HALF, HALF), HALF)].astype(BF16)
-    w_in, b_in = [], []
+    w_in, u_in, b_in = [], [], []
     for d in (4, 3, 5, 2, 6, 1, 7):
         w_in.append(push(wpart.at[z], wpart.at[z], w_s.at[d], w_r.at[d], at(dz=d)))
     t_in.wait_recv()
@@ -324,6 +334,16 @@
         copy.wait_recv()
 
     grad_pre = msg[...].reshape(NC * NY * LAB, FEAT)
+    for copy in reversed(w_in):
+        copy.wait_recv()
+    chunk_sum = wpart[0].astype(F32)
+    for i in range(1, NZ):
+        chunk_sum += wpart[i].astype(F32)
+    ypart[yh, c] = chunk_sum.astype(BF16)
+    for dy, dc in ((2, 1), (2, 0), (1, 1), (3, 1), (1, 0), (3, 0), (0, 1)):
+        u_in.append(push(
+            ypart.at[yh, c], ypart.at[yh, c], u_s.at[dc * NY + dy], u_r.at[dc * NY + dy], at(dy=dy, dc=dc)
+        ))
     grad_agg = lax.dot_general(grad_pre, w, CONTRACT_LANES, preferred_element_type=F32).astype(BF16)
     term = jnp.dot(at8[...].reshape(NZ * ROWS, NC * NY * LAB), grad_agg, preferred_element_type=F32)
     cstage[...] = term.astype(BF16).reshape(NZ, ROWS, FEAT)
@@ -332,21 +352,10 @@
         push(cstage.at[z_at(4), top], z_relay.at[0], f_s.at[0], f_r.at[0], at(dz=3)),
         push(cstage.at[z_at(4), bottom], z_relay.at[1], f_s.at[1], f_r.at[1], at(dz=-3)),
     ]
-    for d in (3, -3, 2, -2):
+    for d in (2, -2, 3, -3):
         b_in.append(push(cstage.at[z_at(d)], cin.at[d % NZ], b_s.at[d % NZ], b_r.at[d % NZ], at(dz=d)))
     b_in.append(push(cstage.at[z_at(1), bottom], cin.at[1, bottom], b_s.at[1], b_r.at[1], at(dz=1)))
     b_in.append(push(cstage.at[z_at(-1), top], cin.at[7, top], b_s.at[7], b_r.at[7], at(dz=-1)))
-    for copy in reversed(w_in):
-        copy.wait_recv()
-    chunk_sum = wpart[0].astype(F32)
-    for i in range(1, NZ):
-        chunk_sum += wpart[i].astype(F32)
-    ypart[yh, c] = chunk_sum.astype(BF16)
-    u_in = []
-    for dy, dc in ((2, 1), (2, 0), (1, 1), (3, 1), (1, 0), (3, 0), (0, 1)):
-        u_in.append(push(
-            ypart.at[yh, c], ypart.at[yh, c], u_s.at[dc * NY + dy], u_r.at[dc * NY + dy], at(dy=dy, dc=dc)
-        ))
     for copy in u_in:
         copy.wait_recv()
     chunk_sum = ypart[0].astype(F32)
@@ -417,7 +426,8 @@
             pltpu.VMEM((NZ, TILE, TILE), BF16),
             pltpu.VMEM((NZ, ROWS, NC * TILE), BF16),
             pltpu.VMEM((NR, NC * REP_HALF, TILE), BF16),
-            pltpu.VMEM((6, REP_HALF, FEAT), BF16),
+            pltpu.VMEM((8, REP_HALF, FEAT), BF16),
+            pltpu.VMEM((REP_HALF, FEAT), F32),
             pltpu.VMEM((2, 2, REP_HALF, TILE), BF16),
             pltpu.VMEM((NC * NY, LAB, FEAT), BF16),
             pltpu.VMEM((NC, LAB, TILE), BF16),
@@ -431,7 +441,7 @@
             dma((10,)),
             dma((4, 2)), dma((4, 2)), dma((4,)), dma((4,)), dma((2, 5, 4)), dma((2, 5, 4)),
             dma((4,)), dma((4,)), dma((1,)), dma((1,)),
-            dma((2, 2)), dma((2, 2)), dma((6, 2)), dma((6, 2)), dma((8,)), dma((8,)), dma((8,)), dma((8,)), dma((8,)), dma((8,)),
+            dma((2, 2)), dma((2, 2)), dma((8, 2)), dma((8, 2)), dma((8,)), dma((8,)), dma((8,)), dma((8,)), dma((8,)), dma((8,)),
             dma((8,)), dma((8,)), dma((4,)), dma((4,)), dma((8,)), dma((8,)),
         ],
         compiler_params=pltpu.CompilerParams(

time: 63.8 us -> 62.2 us (0.975)
  Pallas kernels: 62.3 us -> 60.8 us
    pallas_call x1, Pallas kernels: 60.6 us -> 59.1 us  [per_device(): pl.pallas_call(kernel, name='graph_layer', out_shape=shapes, in_specs=[hb...]
where the time goes in v4:
time: 62.2 us; the launch traced here: 62.1 us
  Pallas kernels  60.8 us (98%)
  between operations  1.29 us (2%)
    pallas_call x1, Pallas kernels, per_device(): pl.pallas_call(kernel, name='graph_layer', out_shape=shapes, in_specs=[hb...  59.1 us
    pallas_call x1, Pallas kernels, per_device(): pl.pallas_call(write_out, name='write_out', out_shape=shapes, in_specs=[v...  1.72 us

profile of v4, /device:TPU:1, one launch (start us, length us, event | category | flops | bytes accessed | tf_op | source)
XLA Modules:
  0.0 62.1 jit_solution(11793129318522991123)
XLA Ops:
  1.3 59.1 %graph_layer.1 = (bf16[64,256]{1,0:T(8,128)(2,1)}, bf16[64,256]{1,0:T(8,128)(2,1)}, f32[256,256]{1,0:T(8,128)}) custom-call(bf16[64,256]{1,0:T(8,128)(2,1)} %feats.1, bf16[256,256]{1,0:T(8,128)(2,1)} %weight.1, bf16[64,128,128]{2,1,0:T(8,128)(2,1)} %values.1, s32[1,64]{1,0:T(1,128)} %bitcast.2, s32[1,64]{1,0:T(1,128)} %bitcast.3, s32[1]{0:T(128)S(6)} %copy.11.tcount_h, ...), custom_call_target="tpu_custom_call" | custom-call | tf_op jit(solution)/shard_map/graph_layer/pallas_call | solution.py:403
  60.3 1.7 %write_out.1 = (bf16[64,256]{1,0:T(8,128)(2,1)}, bf16[64,256]{1,0:T(8,128)(2,1)}, f32[256,256]{1,0:T(8,128)}) custom-call(bf16[64,256]{1,0:T(8,128)(2,1)} %get-tuple-element.6.layer_in, bf16[64,256]{1,0:T(8,128)(2,1)} %get-tuple-element.7.feats_in, f32[256,256]{1,0:T(8,128)} %get-tuple-element.8.weight_in), custom_call_target="tpu_custom_call" | custom-call | tf_op jit(solution)/shard_map/write_out/pallas_call | solution.py:454

commit v5 on v4

--- a/solution.py
+++ b/solution.py
@@ -238,13 +238,7 @@
             stage[i, base:base + ROWS] = low[i * ROWS:(i + 1) * ROWS]
             stage[i, base + ROWS:base + REP_HALF] = picked
     halves = (pl.ds(0, REP_HALF), pl.ds(REP_HALF, REP_HALF))
-    relay, rep_arrivals = {}, []
-    for dyl in (1, 0):
-        for side, dx in ((1, -1),):
-            relay[side, dyl] = push(
-                stage.at[target(2, dyl), halves[side]], relay_in.at[side, dyl],
-                q_s.at[side, dyl], q_r.at[side, dyl], (loop, target(dx, 0)),
-            )
+    rep_arrivals = []
 
     def send_rep(dx, dyl, side):
         to, slot = target(dx, dyl), dyl * 4 + dx + 1
@@ -253,23 +247,11 @@
             rep_s.at[slot, side], rep_r.at[slot, side], (at(dc=side)[0], to),
         ))
 
-    send_rep(2, 1, 0)
-    send_rep(2, 0, 0)
-    send_rep(0, 1, 0)
-    send_rep(0, 1, 1)
-    for dyl in (1, 0):
-        for side, dx in enumerate((1, -1)):
-            send_rep(dx, dyl, 1 - side)
-        send_rep(1, dyl, 0)
+    for dx, dyl in ((2, 1), (2, 0), (1, 1), (-1, 1), (0, 1), (1, 0), (-1, 0)):
+        for side in range(NC):
+            send_rep(dx, dyl, side)
     send_rep(0, 0, 1)
     rep_in[1, :, lanes] = stage[rep, 0:REP_HALF]
-    for dyl in (1, 0):
-        for side, dx in ((1, -1),):
-            relay[side, dyl].wait_recv()
-            to, part = target(dx, dyl), halves[side]
-            merged = stage[to, part].astype(F32) + relay_in[side, dyl].astype(F32)
-            stage[to, part] = merged.astype(BF16)
-            send_rep(dx, dyl, side)
     gather_sends = list(sends)
     for jj in range(1, NY):
         a_in[jj].wait_recv()
@@ -290,11 +272,8 @@
     for copy in rep_arrivals:
         copy.wait_recv()
     total = rep_in[0].astype(F32)
-    for i in (1, 2, 4, 5, 6):
+    for i in range(1, 8):
         total += rep_in[i].astype(F32)
-    total_v[...] = total
-    total_v[:, lanes] += rep_in[3, :, lanes].astype(F32) + rep_in[7, :, lanes].astype(F32)
-    total = total_v[...]
     agg = total.astype(BF16)
     pre = jnp.dot(agg, w, preferred_element_type=F32)
     gate = jax.nn.sigmoid(pre)
@@ -347,15 +326,8 @@
     grad_agg = lax.dot_general(grad_pre, w, CONTRACT_LANES, preferred_element_type=F32).astype(BF16)
     term = jnp.dot(at8[...].reshape(NZ * ROWS, NC * NY * LAB), grad_agg, preferred_element_type=F32)
     cstage[...] = term.astype(BF16).reshape(NZ, ROWS, FEAT)
-    top, bottom = pl.ds(0, ROWS // 2), pl.ds(ROWS // 2, ROWS // 2)
-    far = [
-        push(cstage.at[z_at(4), top], z_relay.at[0], f_s.at[0], f_r.at[0], at(dz=3)),
-        push(cstage.at[z_at(4), bottom], z_relay.at[1], f_s.at[1], f_r.at[1], at(dz=-3)),
-    ]
-    for d in (2, -2, 3, -3):
-        b_in.append(push(cstage.at[z_at(d)], cin.at[d % NZ], b_s.at[d % NZ], b_r.at[d % NZ], at(dz=d)))
-    b_in.append(push(cstage.at[z_at(1), bottom], cin.at[1, bottom], b_s.at[1], b_r.at[1], at(dz=1)))
-    b_in.append(push(cstage.at[z_at(-1), top], cin.at[7, top], b_s.at[7], b_r.at[7], at(dz=-1)))
+    for d in (1, 7, 2, 6, 3, 5, 4):
+        b_in.append(push(cstage.at[z_at(d)], cin.at[d], b_s.at[d], b_r.at[d], at(dz=d)))
     for copy in u_in:
         copy.wait_recv()
     chunk_sum = ypart[0].astype(F32)
@@ -365,15 +337,10 @@
     v_in = []
     for d in (6, 2, 5, 7, 3, 1, 4):
         v_in.append(push(gwbuf.at[rep], gwbuf.at[rep], v_s.at[d], v_r.at[d], at(dr=d)))
-    for i, (d, part) in enumerate(((1, top), (-1, bottom))):
-        far[i].wait_recv()
-        merged = cstage[z_at(d), part].astype(F32) + z_relay[i].astype(F32)
-        cstage[z_at(d), part] = merged.astype(BF16)
-        b_in.append(push(cstage.at[z_at(d), part], cin.at[d % NZ, part], f_s.at[2 + i], f_r.at[2 + i], at(dz=d)))
     total = cstage[z].astype(F32)
     for copy in b_in:
         copy.wait_recv()
-    for d in (1, 2, 3, 5, 6, 7):
+    for d in range(1, NZ):
         total += cin[d].astype(F32)
     grad_feats[...] = total.astype(BF16)
     for copy in sends[len(gather_sends):]:

time: 62.2 us -> 61.1 us (0.982)
  Pallas kernels: 60.8 us -> 59.7 us
    pallas_call x1, Pallas kernels: 59.1 us -> 58 us  [per_device(): pl.pallas_call(kernel, name='graph_layer', out_shape=shapes, in_specs=[hb...]
where the time goes in v5:
time: 61.1 us; the launch traced here: 61 us
  Pallas kernels  59.7 us (98%)
  between operations  1.29 us (2%)
    pallas_call x1, Pallas kernels, per_device(): pl.pallas_call(kernel, name='graph_layer', out_shape=shapes, in_specs=[hb...  58 us
    pallas_call x1, Pallas kernels, per_device(): pl.pallas_call(write_out, name='write_out', out_shape=shapes, in_specs=[v...  1.72 us

profile of v5, /device:TPU:1, one launch (start us, length us, event | category | flops | bytes accessed | tf_op | source)
XLA Modules:
  0.0 61.0 jit_solution(7434972308024911641)
XLA Ops:
  1.3 58.0 %graph_layer.1 = (bf16[64,256]{1,0:T(8,128)(2,1)}, bf16[64,256]{1,0:T(8,128)(2,1)}, f32[256,256]{1,0:T(8,128)}) custom-call(bf16[64,256]{1,0:T(8,128)(2,1)} %feats.1, bf16[256,256]{1,0:T(8,128)(2,1)} %weight.1, bf16[64,128,128]{2,1,0:T(8,128)(2,1)} %values.1, s32[1,64]{1,0:T(1,128)} %bitcast.2, s32[1,64]{1,0:T(1,128)} %bitcast.3, s32[1]{0:T(128)S(6)} %copy.11.tcount_h, ...), custom_call_target="tpu_custom_call" | custom-call | tf_op jit(solution)/shard_map/graph_layer/pallas_call | solution.py:370
  59.3 1.7 %write_out.1 = (bf16[64,256]{1,0:T(8,128)(2,1)}, bf16[64,256]{1,0:T(8,128)(2,1)}, f32[256,256]{1,0:T(8,128)}) custom-call(bf16[64,256]{1,0:T(8,128)(2,1)} %get-tuple-element.6.layer_in, bf16[64,256]{1,0:T(8,128)(2,1)} %get-tuple-element.7.feats_in, f32[256,256]{1,0:T(8,128)} %get-tuple-element.8.weight_in), custom_call_target="tpu_custom_call" | custom-call | tf_op jit(solution)/shard_map/write_out/pallas_call | solution.py:421
